TPU v7x, 128 devices: a whole 4x4x4 slice. The times are simulated.
128 devices in a mesh: grp: 16 (over z, y), own: 8 (over x, core).
Axes of the slice: x: 4, y: 4, z: 4, core: 2. Of those that a mesh axis runs over, the one named last changes fastest.
Arguments:
- queries: bfloat16 [4096, 1024], P(('grp', 'own')), may hold values from -20 to 20
- centroids: bfloat16 [32768, 1024], P('own'), may hold values from -6 to 6
- cluster_ids: int32 [4096, 8], P(('grp', 'own')), may hold values from 0 to 255, all different within a row; in each aligned block of 32 rows (0 to 31, 32 to 63, ...) at most 2 rows name the same one
- label_weights: bfloat16 [256, 3072, 1024], P(('grp', 'own')), may hold values from -6 to 6
Outputs:
- label_logp: float32 [4096, 8, 3072], P(('grp', 'own'))
Inputs may be any that keep to these rules, and one draw needn't show every extreme that they name: `cluster_ids`: each row names 8 different clusters; among the rows of one device no cluster is named by more than 2 rows, a bound that some block reaches.
All inputs are finite; a program needn't handle non-finite values.
Results may differ from a plain program's by a relative error of at most 0.0003.
Values may be sent and summed in bfloat16 or wider, within the bound.
No kernel may reach another device: no remote copies, remote signals or barrier semaphores. Data moves between devices by JAX's collectives and lax.ppermute only.
A program may use at most 128 MiB of HBM per device.

v0:
```python
import jax
import jax.numpy as jnp
from jax import lax
from jax.sharding import PartitionSpec as P


def owner_scores(arrived, label_weights):
    logits = jnp.einsum(
        "scmd,cld->scml", arrived, label_weights, preferred_element_type=jnp.float32
    )
    largest = jnp.max(logits, axis=-1)
    log_total = largest + jnp.log(jnp.sum(jnp.exp(logits - largest[..., None]), axis=-1))
    return (logits.astype(jnp.bfloat16), log_total)


def body(queries, centroids, cluster_ids, label_weights):
    rows_here, width = queries.shape
    beam_width = cluster_ids.shape[1]
    group_size = lax.axis_size("grp")
    owner_count = lax.axis_size("own")
    devices = group_size * owner_count
    held_clusters = label_weights.shape[0]
    label_count = label_weights.shape[1]
    window_clusters = held_clusters * devices
    held_centroids = centroids.shape[0]
    spacing = held_centroids * owner_count // window_clusters
    local_heads = held_centroids // spacing
    capacity = 2 * rows_here * beam_width // window_clusters
    first_centroid = lax.axis_index("own") * held_centroids
    head_index = jnp.arange(local_heads, dtype=jnp.int32)
    piece_queries = lax.all_gather(queries, "own", axis=0, tiled=True)
    piece_ids = lax.all_gather(cluster_ids, "own", axis=0, tiled=True)
    scores = jnp.dot(piece_queries, centroids.T, preferred_element_type=jnp.float32)
    local_max = jnp.max(scores, axis=1)
    local_sum = jnp.sum(jnp.exp(scores - local_max[:, None]), axis=1)
    heads = scores.reshape(scores.shape[0], local_heads, spacing)[:, :, 0]
    offset = piece_ids * spacing - first_centroid
    position = jnp.where(offset >= 0, offset // spacing, -1)
    match = position[:, :, None] == head_index[None, None, :]
    picked = jnp.sum(jnp.where(match, heads[:, None, :], 0.0), axis=2)
    maxima = local_max
    totals = local_sum
    picks = picked
    top_max = lax.pmax(maxima, "own")
    totals, picks = lax.psum((totals * jnp.exp(maxima - top_max), picks), "own")
    maxima = top_max
    prior_group = picks - (maxima + jnp.log(totals))[:, None]
    prior = lax.dynamic_slice_in_dim(prior_group, lax.axis_index("own") * rows_here, rows_here, 0)
    clusters = jnp.arange(window_clusters, dtype=jnp.int32)
    named = cluster_ids[:, :, None] == clusters[None, None, :]
    hits = jnp.any(named, axis=1).astype(jnp.int32)
    before = jnp.cumsum(hits, axis=0) - hits
    slot_rank = jnp.sum(jnp.where(named, before[:, None, :], 0), axis=2)
    places = jnp.arange(capacity, dtype=jnp.int32)
    select = ((before.T[:, None, :] == places[None, :, None]) & (hits.T[:, None, :] == 1)).astype(
        jnp.bfloat16
    )
    outgoing = jnp.einsum(
        "wmq,qd->wmd", select, queries, preferred_element_type=jnp.float32
    ).astype(jnp.bfloat16)
    outgoing = outgoing.reshape(devices, held_clusters, capacity, width)
    logits, log_total = owner_scores(
        lax.all_to_all(outgoing, ("grp", "own"), split_axis=0, concat_axis=0, tiled=True),
        label_weights,
    )
    scores_home = lax.all_to_all(
        logits.astype(jnp.float32), ("grp", "own"), split_axis=0, concat_axis=0, tiled=True
    ).astype(logits.dtype)
    totals_home = lax.all_to_all(log_total, ("grp", "own"), split_axis=0, concat_axis=0, tiled=True)
    flat_index = (cluster_ids * capacity + slot_rank).reshape(-1)
    slot_count = window_clusters * capacity
    slot_index = jnp.arange(slot_count, dtype=jnp.int32)
    onehot = flat_index[:, None] == slot_index[None, :]
    picked = jnp.dot(
        onehot.astype(jnp.bfloat16),
        scores_home.reshape(slot_count, label_count),
        preferred_element_type=jnp.float32,
    )
    picked = picked.reshape(rows_here, beam_width, label_count)
    chosen_totals = jnp.sum(jnp.where(onehot, totals_home.reshape(1, slot_count), 0.0), axis=1)
    chosen_totals = chosen_totals.reshape(rows_here, beam_width)
    return prior[:, :, None] + picked - chosen_totals[:, :, None]


def solution(mesh):
    placed = (
        P(("grp", "own"), None),
        P("own", None),
        P(("grp", "own"), None),
        P(("grp", "own"), None, None),
    )
    return jax.shard_map(
        body, mesh=mesh, in_specs=placed, out_specs=P(("grp", "own"), None, None), check_vma=False
    )
```

profile of v0, /device:TPU:1, one launch (start us, length us, event | category | flops | bytes accessed | tf_op | source)
XLA Modules:
  0.0 174.8 jit_solution(10988242132317876631)
XLA Ops:
  0.0 0.8 copy.43
  0.8 0.2 fusion.10
  0.9 0.1 reduce_window_sum.11
  1.0 1.3 convolution_convert_fusion
  2.3 1.1 copy.50
  3.4 30.8 %all_to_all.15 = bf16[128,2,2,1024]{3,2,1,0:T(2,128)(2,1)} all-to-all(bf16[128,2,2,1024]{3,2,1,0:T(2,128)(2,1)S(1)} %bitcast.39), channel_id=1, replica_groups=mesh['grp'=16,'own'=8] {'grp','own'}, dimensions={0} | all-to-all | bytes 2097152 | tf_op jit(solution)/shard_map/all_to_all | solution.py:63
  34.2 10.1 %fusion.5 = (bf16[128,2,2,3072]{3,0,2,1:T(8,128)(2,1)}, f32[2,128,2,3072]{3,1,2,0:T(8,128)S(1)}) fusion(bf16[2,3072,1024]{2,1,0:T(8,128)(2,1)} %param.7, bf16[128,2,2,1024]{3,2,1,0:T(2,128)(2,1)} %all_to_all.15), kind=kOutput, calls=%fused_computation.10 | convolution fusion | flops 3222798336 | bytes 23068672 | tf_op jit(solution)/shard_map/scmd,cld->scml/dot_general | solution.py:8
  44.3 0.4 bitcast_reduce_fusion
  44.7 1.0 fusion.3
  45.7 0.8 copy.48
  46.5 4.3 %all-to-all-start.2 = ((f32[128,2,2]{2,1,0:T(2,128)}), f32[128,2,2]{2,1,0:T(2,128)S(1)}, u32[]{:S(2)}, u32[]{:S(2)}) async-start(f32[128,2,2]{2,1,0:T(2,128)} %copy.48), calls=%async_computation.2 | async-start | bytes 262144 | tf_op jit(solution)/shard_map/all_to_all | solution.py:69
  50.8 6.9 %copy.47 = bf16[128,2,2,3072]{3,2,1,0:T(2,128)(2,1)} copy(bf16[128,2,2,3072]{3,0,2,1:T(8,128)(2,1)} %get-tuple-element.9) | data formatting | bytes 6291456 | tf_op jit(solution)/shard_map/convert_element_type | solution.py:67
  57.7 0.0 copy-start.1
  57.7 3.2 %all-to-all-done.2 = f32[128,2,2]{2,1,0:T(2,128)S(1)} async-done(((f32[128,2,2]{2,1,0:T(2,128)}), f32[128,2,2]{2,1,0:T(2,128)S(1)}, u32[]{:S(2)}, u32[]{:S(2)}) %all-to-all-start.2) | async-done | bytes 2080 | tf_op jit(solution)/shard_map/all_to_all | solution.py:69
  60.9 6.6 %all-to-all-start.1 = ((bf16[128,2,2,3072]{3,2,1,0:T(2,128)(2,1)}), bf16[128,2,2,3072]{3,2,1,0:T(2,128)(2,1)S(1)}, u32[]{:S(2)}, u32[]{:S(2)}) async-start(bf16[128,2,2,3072]{3,2,1,0:T(2,128)(2,1)} %copy.47), calls=%async_computation.1 | async-start | bytes 6291456 | tf_op jit(solution)/shard_map/all_to_all | solution.py:66
  67.6 0.7 select_reduce_fusion.1
  68.3 0.1 eq.102
  68.4 0.0 copy-done.1
  68.4 44.3 %all_gather.7 = bf16[256,1024]{1,0:T(8,128)(2,1)S(1)} all-gather(bf16[32,1024]{1,0:T(8,128)(2,1)S(1)} %copy-done.1), channel_id=1, replica_groups=mesh['grp'=16,'own'=8] {'own'}, dimensions={0}, use_global_device_ids=true | all-gather | bytes 589824 | tf_op jit(solution)/shard_map/all_gather | solution.py:31
  112.7 5.8 %fusion.19 = (f32[256]{0:T(256)S(1)}, f32[256,4096]{1,0:T(8,128)S(1)}) fusion(bf16[256,1024]{1,0:T(8,128)(2,1)S(1)} %all_gather.7, bf16[4096,1024]{1,0:T(8,128)(2,1)} %param.5), kind=kOutput, calls=%fused_computation.44 | convolution fusion | flops 2148531968 | bytes 13108224 | tf_op jit(solution)/shard_map/dot_general | solution.py:33
  118.5 0.0 copy-start
  118.6 3.1 %copy.52 = f32[32,8,32,128]{3,2,1,0:T(8,128)} copy(f32[32,8,32,128]{3,1,2,0:T(8,128)S(1)} %bitcast.37) | data formatting | bytes 8388608
  121.7 0.1 copy-done
  121.8 0.0 copy-start.2
  121.8 3.6 %copy.51 = f32[256,32,1]{0,1,2:T(8,128)S(1)} copy(f32[256,32,1]{2,1,0:T(8,128)} %bitcast.38) | data formatting | bytes 65536
  125.3 0.0 copy-done.2
  125.4 12.8 %all-gather = s32[8,32,8]{1,2,0:T(8,128)S(1)} all-gather(s32[1,32,8]{1,2,0:T(8,128)S(1)} %bitcast.42), channel_id=1, replica_groups=mesh['grp'=16,'own'=8] {'own'}, dimensions={0}, use_global_device_ids=true | all-gather | bytes 9216 | tf_op jit(solution)/shard_map/all_gather | solution.py:32
  138.2 0.1 reshape.59
  138.2 12.0 %pmax.7 = f32[256]{0:T(256)S(1)} all-reduce(f32[256]{0:T(256)S(1)} %get-tuple-element.11), channel_id=1, replica_groups=mesh['grp'=16,'own'=8] {'own'}, use_global_device_ids=true, to_apply=%region_3.4 | all-reduce | flops 256 | bytes 2048 | tf_op jit(solution)/shard_map/pmax | solution.py:44
  150.3 2.9 %exponential_reduce_fusion = f32[256]{0:T(256)S(1)} fusion(f32[256,4096]{1,0:T(8,128)} %copy-done, f32[256]{0:T(256)S(1)} %get-tuple-element.11), kind=kLoop, calls=%fused_computation.7 | loop fusion | flops 2096896 | bytes 4196352 | tf_op jit(solution)/shard_map/reduce_sum | solution.py:35
  153.2 13.5 %all-reduce = (f32[256,8]{0,1:T(8,128)S(1)}, f32[256]{0:T(256)S(1)}) all-reduce(f32[256,8]{0,1:T(8,128)S(1)} %select_reduce_fusion.2, f32[256]{0:T(256)S(1)} %exponential_multiply_fusion), channel_id=1, replica_groups=mesh['grp'=16,'own'=8] {'own'}, use_global_device_ids=true, to_apply=%region_1.0 | all-reduce | flops 2304 | bytes 18432 | tf_op jit(solution)/shard_map/psum | solution.py:45
  166.7 0.1 dynamic-slice
  166.8 0.1 dynamic-slice_subtract_fusion
  166.9 0.1 copy.42
  167.0 0.2 broadcast_in_dim.60
  167.1 0.2 select_reduce_fusion
  167.3 0.1 sub.72
  167.4 0.0 all-to-all-done.1
  167.4 2.7 %reshape.62 = bf16[512,3072,1]{1,0,2:T(8,128)(2,1)} reshape(bf16[128,2,2,3072]{3,2,1,0:T(2,128)(2,1)S(1)} %all-to-all-done.1) | data formatting | bytes 6291456 | tf_op jit(solution)/shard_map/reshape | solution.py:76
  170.2 4.6 %fusion.4 = f32[32,8,3072]{2,1,0:T(8,128)} fusion(bf16[512,3072,1]{1,0,2:T(8,128)(2,1)} %reshape.62, f32[32,8]{1,0:T(8,128)S(1)} %sub.72, f32[32,8]{1,0:T(8,128)S(1)} %copy.42, s32[32,8]{1,0:T(8,128)S(1)} %multiply_add_fusion), kind=kOutput, calls=%fused_computation.9 | convolution fusion | flops 807010304 | bytes 6294528 | tf_op jit(solution)/shard_map/dot_general | solution.py:74
  (10 shorter events, 0.1 us)
Async XLA Ops:
  46.5 14.5 %all-to-all-start.2 = ((f32[128,2,2]{2,1,0:T(2,128)}), f32[128,2,2]{2,1,0:T(2,128)S(1)}, u32[]{:S(2)}, u32[]{:S(2)}) async-start(f32[128,2,2]{2,1,0:T(2,128)} %copy.48), calls=%async_computation.2 | async-start | bytes 262144 | tf_op jit(solution)/shard_map/all_to_all | solution.py:69
  57.7 10.7 %copy-start.1 = (bf16[32,1024]{1,0:T(8,128)(2,1)S(1)}, bf16[32,1024]{1,0:T(8,128)(2,1)}, u32[]{:S(2)}) copy-start(bf16[32,1024]{1,0:T(8,128)(2,1)} %param.4) | copy-start | bytes 196612
  60.9 106.5 %all-to-all-start.1 = ((bf16[128,2,2,3072]{3,2,1,0:T(2,128)(2,1)}), bf16[128,2,2,3072]{3,2,1,0:T(2,128)(2,1)S(1)}, u32[]{:S(2)}, u32[]{:S(2)}) async-start(bf16[128,2,2,3072]{3,2,1,0:T(2,128)(2,1)} %copy.47), calls=%async_computation.1 | async-start | bytes 6291456 | tf_op jit(solution)/shard_map/all_to_all | solution.py:66
  118.5 3.2 %copy-start = (f32[256,4096]{1,0:T(8,128)}, f32[256,4096]{1,0:T(8,128)S(1)}, u32[]{:S(2)}) copy-start(f32[256,4096]{1,0:T(8,128)S(1)} %get-tuple-element.12) | copy-start | bytes 12582916
  121.8 3.6 %copy-start.2 = (s32[32,8]{0,1:T(8,128)S(1)}, s32[32,8]{0,1:T(8,128)}, u32[]{:S(2)}) copy-start(s32[32,8]{0,1:T(8,128)} %param.6) | copy-start | bytes 3076
where the time goes:
time: 175 us
  blocking collectives  113 us (65%)
  matrix products  21.9 us (13%)
  local copies, waits for them, and re-layouts  19.6 us (11%)
  starting transfers between devices  11 us (6%)
  other arithmetic  5.54 us (3%)
  waiting for transfers between devices  3.24 us (2%)
    all_gather x1, blocking collectives, body(): piece_queries = lax.all_gather(queries, 'own', axis=0, tiled=True)  44.3 us
    all_to_all x1, blocking collectives, body(): lax.all_to_all(outgoing, ('grp', 'own'), split_axis=0, concat_axis=0, til...  30.8 us
    psum x1, blocking collectives, body(): totals, picks = lax.psum((totals * jnp.exp(maxima - top_max), picks), 'own')  13.5 us
    all_gather x1, blocking collectives, body(): piece_ids = lax.all_gather(cluster_ids, 'own', axis=0, tiled=True)  12.8 us
    pmax x1, blocking collectives, body(): top_max = lax.pmax(maxima, 'own')  12 us
    dot_general x1, matrix products, owner_scores(): jnp.einsum('scmd,cld->scml', arrived, label_weights, preferred_element_ty...  10.1 us
    unnamed x9, local copies, waits for them, and re-layouts  7.56 us
    convert_element_type x1, local copies, waits for them, and re-layouts, body(): logits.astype(jnp.float32)  6.88 us
  transfers between devices with their start and end apart: 2, of which 1 were waited for; matrix products, arithmetic and copies ran while one was open for 14% of the time, Pallas kernels for 0%

commit v1 on v0

v1 whole, which is shorter than its diff:
```python
import functools

import jax
import jax.numpy as jnp
from jax import lax
from jax.experimental import pallas as pl
from jax.experimental.pallas import tpu as pltpu
from jax.sharding import PartitionSpec as P

LANES = 128
F32, BF16 = jnp.float32, jnp.bfloat16
MIB = 1 << 20


def route_kernel(clusters, capacity, queries_hbm, ids_hbm, out_ref, slot_ref, queries_ref, ids_ref, stage, sems):
    copies = [
        pltpu.make_async_copy(ids_hbm, ids_ref, sems.at[0]),
        pltpu.make_async_copy(queries_hbm, queries_ref, sems.at[1]),
    ]
    for copy in copies:
        copy.start()
    copies[0].wait()
    rows, width = queries_ref.shape
    beam = ids_ref.shape[0]
    tiles = width // LANES
    cluster = lax.broadcasted_iota(jnp.int32, (clusters, rows), 0)
    named = [cluster == ids_ref[s : s + 1, :] for s in range(beam)]
    hits = functools.reduce(jnp.logical_or, named)
    earlier = lax.broadcasted_iota(jnp.int32, (rows, rows), 0) < lax.broadcasted_iota(
        jnp.int32, (rows, rows), 1
    )
    before = jnp.dot(
        jnp.where(hits, 1.0, 0.0).astype(BF16),
        jnp.where(earlier, 1.0, 0.0).astype(BF16),
        preferred_element_type=F32,
    )
    copies[1].wait()
    for m in range(capacity):
        select = jnp.where(hits & (before == m), 1.0, 0.0).astype(BF16)
        routed = jnp.dot(select, queries_ref[...], preferred_element_type=F32)
        for k in range(tiles):
            stage[pl.ds(m * tiles + k, clusters, stride=capacity * tiles), :] = routed[
                :, k * LANES : (k + 1) * LANES
            ]
    out_ref[...] = stage[...].astype(BF16)
    rank = jnp.concatenate(
        [jnp.sum(jnp.where(n, before, 0.0), axis=0, keepdims=True) for n in named], axis=0
    )
    slot_ref[...] = ids_ref[...] * capacity + rank.astype(jnp.int32)


def route(queries, ids, clusters, capacity):
    rows, width = queries.shape
    total = clusters * capacity * width // LANES
    return pl.pallas_call(
        functools.partial(route_kernel, clusters, capacity),
        out_shape=(
            jax.ShapeDtypeStruct((total, LANES), BF16),
            jax.ShapeDtypeStruct(ids.shape, jnp.int32),
        ),
        in_specs=[pl.BlockSpec(memory_space=pltpu.HBM)] * 2,
        scratch_shapes=[
            pltpu.VMEM(queries.shape, BF16),
            pltpu.VMEM(ids.shape, jnp.int32),
            pltpu.VMEM((total, LANES), F32),
            pltpu.SemaphoreType.DMA((2,)),
        ],
        compiler_params=pltpu.CompilerParams(vmem_limit_bytes=56 * MIB),
        name="route",
    )(queries, ids)


def label_kernel(sources, capacity, arrived_ref, weights_ref, out_ref, spread, x, w, logits, stage, pack, sems, out_sems):
    held, labels, width = weights_ref.shape
    tiles, columns = width // LANES, labels // LANES
    rows = stage.shape[0] // sources
    blocks = w.shape[1]
    block = labels // blocks
    here = block // LANES
    parts = out_sems.shape[0]
    count = sources // parts

    copies = {
        (c, n): pltpu.make_async_copy(weights_ref.at[c, pl.ds(n * block, block)], w.at[c, n], sems.at[c, n])
        for c in range(held)
        for n in range(blocks)
    }
    for copy in copies.values():
        copy.start()
    spread[...] = arrived_ref[...].astype(F32)

    def gather(c):
        for m in range(capacity):
            for k in range(tiles):
                x[c, m * sources : (m + 1) * sources, k * LANES : (k + 1) * LANES] = spread[
                    pl.ds((c * capacity + m) * tiles + k, sources, stride=held * capacity * tiles), :
                ].astype(BF16)

    def product(c, n):
        copies[c, n].wait()
        scores = lax.dot_general(x[c], w[c, n], (((1,), (1,)), ((), ())), preferred_element_type=F32)
        logits[c, :, n * block : (n + 1) * block] = scores
        for m in range(capacity):
            for j in range(here):
                stage[pl.ds((c * capacity + m) * columns + n * here + j, sources, stride=rows), :] = scores[
                    m * sources : (m + 1) * sources, j * LANES : (j + 1) * LANES
                ]

    def total(c, m, p):
        scores = logits[c, m * sources + p * count : m * sources + (p + 1) * count, :]
        largest = jnp.max(scores, axis=1, keepdims=True)
        return largest + jnp.log(jnp.sum(jnp.exp(scores - largest), axis=1, keepdims=True))

    totals = {}
    places = held * capacity
    for c in range(held):
        gather(c)
        for n in range(blocks):
            product(c, n)
            if c > 0:
                for p in range(n * parts // blocks, (n + 1) * parts // blocks):
                    for m in range(capacity):
                        totals[c - 1, m, p] = total(c - 1, m, p)

    lane = lax.broadcasted_iota(jnp.int32, (count, LANES), 1)
    outs = []
    for p in range(parts):
        for m in range(capacity):
            totals[held - 1, m, p] = total(held - 1, m, p)
        packed = jnp.zeros((count, LANES), F32)
        for c in range(held):
            for m in range(capacity):
                rest = totals[c, m, p]
                for t in range(3):
                    term = rest.astype(BF16).astype(F32)
                    packed = jnp.where(lane == t * places + c * capacity + m, term, packed)
                    rest = rest - term
        stage[pl.ds(p * count * rows + places * columns, count, stride=rows), :] = packed
        stage[pl.ds(p * count * rows + places * columns + 1, count, stride=rows), :] = jnp.zeros_like(packed)
        span = pl.ds(p * count * rows, count * rows)
        pack[span, :] = stage[span, :].astype(BF16)
        out = pltpu.make_async_copy(pack.at[span], out_ref.at[span], out_sems.at[p])
        out.start()
        outs.append(out)
    for out in outs:
        out.wait()


def score_labels(arrived, weights, sources, capacity):
    held, labels, width = weights.shape
    slots = sources * capacity
    blocks = 2
    rows = held * capacity * labels // LANES + 2
    return pl.pallas_call(
        functools.partial(label_kernel, sources, capacity),
        in_specs=[pl.BlockSpec(memory_space=pltpu.VMEM), pl.BlockSpec(memory_space=pltpu.HBM)],
        out_specs=pl.BlockSpec(memory_space=pltpu.HBM),
        out_shape=jax.ShapeDtypeStruct((sources * rows, LANES), BF16),
        scratch_shapes=[
            pltpu.VMEM(arrived.shape, F32),
            pltpu.VMEM((held, slots, width), BF16),
            pltpu.VMEM((held, blocks, labels // blocks, width), BF16),
            pltpu.VMEM((held, slots, labels), F32),
            pltpu.VMEM((sources * rows, LANES), F32),
            pltpu.VMEM((sources * rows, LANES), BF16),
            pltpu.SemaphoreType.DMA((held, blocks)),
            pltpu.SemaphoreType.DMA((4,)),
        ],
        compiler_params=pltpu.CompilerParams(vmem_limit_bytes=54 * MIB),
        cost_estimate=pl.CostEstimate(
            flops=2 * held * slots * labels * width,
            bytes_accessed=2 * held * labels * width,
            transcendentals=held * slots * labels,
        ),
        name="score_labels",
    )(arrived, weights)


def centroid_kernel(spacing, *refs):
    chips = (len(refs) - 7) // 2
    mine_refs, theirs_ref, centroids_ref, out_refs = refs[:chips], refs[chips], refs[chips + 1], refs[chips + 2 : -5]
    x, w, scores, heads, sems = refs[-5:]
    blocks, block, _ = w.shape
    here = block // spacing
    held = heads.shape[0]
    rows = mine_refs[0].shape[0]
    copies = [
        pltpu.make_async_copy(centroids_ref.at[pl.ds(n * block, block)], w.at[n], sems.at[n]) for n in range(blocks)
    ]
    for copy in copies:
        copy.start()
    for i, ref in enumerate(mine_refs):
        x[2 * i * rows : (2 * i + 1) * rows, :] = ref[...]
        x[(2 * i + 1) * rows : (2 * i + 2) * rows, :] = theirs_ref[i * rows : (i + 1) * rows, :]
    for n in range(blocks):
        copies[n].wait()
        scores[:, n * block : (n + 1) * block] = lax.dot_general(
            x[...], w[n], (((1,), (1,)), ((), ())), preferred_element_type=F32
        )
        for h in range(here):
            heads[n * here + h : n * here + h + 1, :] = w[n, h * spacing : h * spacing + 16, :].astype(F32)[0:1]
    picked = lax.dot_general(x[...], heads[...].astype(BF16), (((1,), (1,)), ((), ())), preferred_element_type=F32)
    lane = lax.broadcasted_iota(jnp.int32, (2 * rows, LANES), 1)
    for i, ref in enumerate(out_refs):
        span = slice(2 * i * rows, 2 * (i + 1) * rows)
        part = scores[span, :]
        largest = jnp.max(part, axis=1, keepdims=True)
        summed = jnp.sum(jnp.exp(part - largest), axis=1, keepdims=True)
        padded = jnp.concatenate([picked[span], jnp.zeros((2 * rows, LANES - held), F32)], axis=1)
        ref[...] = jnp.where(lane == held, largest, jnp.where(lane == held + 1, summed, padded))


def score_centroids(mine, theirs, centroids, spacing):
    rows, width = mine[0].shape
    held = centroids.shape[0]
    chips = len(mine)
    total = 2 * rows * chips
    blocks = 2
    whole = pl.BlockSpec(memory_space=pltpu.VMEM)
    return pl.pallas_call(
        functools.partial(centroid_kernel, spacing),
        in_specs=[whole] * (chips + 1) + [pl.BlockSpec(memory_space=pltpu.HBM)],
        out_specs=[whole] * chips,
        out_shape=[jax.ShapeDtypeStruct((2 * rows, LANES), F32)] * chips,
        scratch_shapes=[
            pltpu.VMEM((total, width), BF16),
            pltpu.VMEM((blocks, held // blocks, width), BF16),
            pltpu.VMEM((total, held), F32),
            pltpu.VMEM((held // spacing, width), F32),
            pltpu.SemaphoreType.DMA((blocks,)),
        ],
        compiler_params=pltpu.CompilerParams(vmem_limit_bytes=54 * MIB),
        cost_estimate=pl.CostEstimate(
            flops=2 * total * held * width, bytes_accessed=2 * held * width, transcendentals=total * held
        ),
        name="score_centroids",
    )(*mine, theirs, centroids)


def prior_kernel(heads, owner_ref, ids_ref, *refs):
    *share_refs, out_ref = refs
    beam, rows, _ = out_ref.shape
    lane = lax.broadcasted_iota(jnp.int32, (rows, LANES), 1)
    shares = [ref[i * rows : (i + 1) * rows, :] for ref in share_refs for i in range(ref.shape[0] // rows)]
    largest = functools.reduce(jnp.maximum, [v[:, heads : heads + 1] for v in shares])
    summed = sum(v[:, heads + 1 : heads + 2] * jnp.exp(v[:, heads : heads + 1] - largest) for v in shares)
    normalizer = largest + jnp.log(summed)
    ids = ids_ref[...]
    for s in range(beam):
        here = jnp.zeros((rows, LANES), F32)
        for o, v in enumerate(shares):
            at = ids[:, s : s + 1] - owner_ref[o] * heads
            here += jnp.where((lane == at) & (lane < heads), v, 0.0)
        picked = jnp.sum(here, axis=1, keepdims=True)
        out_ref[s] = jnp.broadcast_to(picked - normalizer, (rows, LANES))


def priors(owners, ids, shares, heads):
    rows, beam = ids.shape
    whole = pl.BlockSpec(memory_space=pltpu.VMEM)
    return pl.pallas_call(
        functools.partial(prior_kernel, heads),
        in_specs=[pl.BlockSpec(memory_space=pltpu.SMEM)] + [whole] * (1 + len(shares)),
        out_specs=whole,
        out_shape=jax.ShapeDtypeStruct((beam, rows, LANES), F32),
        compiler_params=pltpu.CompilerParams(vmem_limit_bytes=4 * MIB),
        name="priors",
    )(owners, ids, *shares)


def join_kernel(capacity, columns, slot_ref, prior_ref, scores_ref, out_ref, total_b, wide, ready, sems):
    beam, queries, _ = prior_ref.shape
    per_owner, sources, _ = total_b.shape
    rows = scores_ref.shape[0] // sources
    spans = 8
    span = scores_ref.shape[0] // spans
    for i in range(spans):
        wide[i * span : (i + 1) * span, :] = scores_ref[i * span : (i + 1) * span, :].astype(F32)
    terms = wide[pl.ds(per_owner * columns, sources, stride=rows), :]
    for j in range(per_owner):
        total = sum(terms[:, t * per_owner + j : t * per_owner + j + 1] for t in range(3))
        total_b[j] = jnp.broadcast_to(total, (sources, LANES))

    parts = sems.shape[0]
    block = queries // parts

    def copy(g):
        here = pl.ds(pl.multiple_of(g * block * beam * columns, 8), block * beam * columns)
        return pltpu.make_async_copy(ready.at[here], out_ref.at[here], sems.at[g])

    @pl.loop(0, parts)
    def _(g):
        for i in range(block):
            q = g * block + i
            for s in range(beam):
                slot = slot_ref[s, q]
                source = slot // per_owner
                place = slot % per_owner
                row = wide[pl.ds(source * rows + place * columns, columns), :]
                shift = prior_ref[s, pl.ds(q, 1), :] - total_b[place, pl.ds(source, 1), :]
                ready[pl.ds(q * beam * columns + s, columns, stride=beam), :] = row + shift
        copy(g).start()

    @pl.loop(0, parts)
    def _(g):
        copy(g).wait()


def join(slots, prior, scores, capacity, held, labels):
    beam, queries = slots.shape
    columns = labels // LANES
    places = held * capacity
    sources = scores.shape[0] // (places * columns + 2)
    whole = pl.BlockSpec(memory_space=pltpu.VMEM)
    out = pl.pallas_call(
        functools.partial(join_kernel, capacity, columns),
        in_specs=[pl.BlockSpec(memory_space=pltpu.SMEM)] + [whole] * 2,
        out_specs=pl.BlockSpec(memory_space=pltpu.HBM),
        out_shape=jax.ShapeDtypeStruct((queries * beam * columns, LANES), F32),
        scratch_shapes=[
            pltpu.VMEM((places, sources, LANES), F32),
            pltpu.VMEM(scores.shape, F32),
            pltpu.VMEM((queries * beam * columns, LANES), F32),
            pltpu.SemaphoreType.DMA((8,)),
        ],
        compiler_params=pltpu.CompilerParams(vmem_limit_bytes=24 * MIB),
        name="join",
    )(slots, prior, scores)
    return out.reshape(queries, columns, beam, LANES).transpose(0, 2, 1, 3).reshape(queries, beam, labels)


def exchange(x, axes):
    return lax.all_to_all(x, axes, split_axis=0, concat_axis=0, tiled=True)


def shift(x, by):
    owners = lax.axis_size("own")
    return lax.ppermute(x, "own", [(i, (i + by) % owners) for i in range(owners)])


def swap(x):
    return lax.ppermute(x, "own", [(i, i ^ 1) for i in range(lax.axis_size("own"))])


def body(queries, centroids, cluster_ids, label_weights):
    rows, width = queries.shape
    beam = cluster_ids.shape[1]
    owners = lax.axis_size("own")
    devices = lax.axis_size("grp") * owners
    held, labels, _ = label_weights.shape
    clusters = held * devices
    capacity = 2 * rows * beam // clusters
    spacing = centroids.shape[0] * owners // clusters
    heads = centroids.shape[0] // spacing
    everyone = ("grp", "own")
    hops = range(2, owners, 2)

    mine = [queries] + [shift(queries, by) for by in hops]
    outgoing, slots = route(queries, cluster_ids.T, clusters, capacity)
    outgoing, *mine = lax.optimization_barrier((outgoing, *mine))
    arrived = exchange(outgoing, everyone)

    theirs = swap(jnp.concatenate(mine, axis=0))
    shares = score_centroids(mine, theirs, centroids, spacing)
    arrived, _ = lax.optimization_barrier((arrived, shares[0]))
    back = [shares[0]] + [shift(share, -by) for share, by in zip(shares[1:], hops)]

    scores = score_labels(arrived, label_weights, devices, capacity)
    scores, *back = lax.optimization_barrier((scores, *back))
    pairs = labels * held * capacity // LANES // 2 + 1
    scores_home = exchange(scores.reshape(devices, pairs, 2, LANES), everyone).reshape(scores.shape)

    mate = swap(jnp.concatenate([share[rows:] for share in back], axis=0))
    here = lax.axis_index("own")
    steps = jnp.arange(0, owners, 2, dtype=jnp.int32)
    shard = jnp.concatenate([(here + steps) % owners, ((here ^ 1) + steps) % owners]).astype(jnp.int32)
    prior = priors(shard, cluster_ids, [share[:rows] for share in back] + [mate], heads)
    return join(slots, prior, scores_home, capacity, held, labels)


def solution(mesh):
    placed = (
        P(("grp", "own"), None),
        P("own", None),
        P(("grp", "own"), None),
        P(("grp", "own"), None, None),
    )
    return jax.shard_map(
        body, mesh=mesh, in_specs=placed, out_specs=P(("grp", "own"), None, None), check_vma=False
    )
```

time: 175 us -> 103 us (0.59)
  blocking collectives: 113 us -> 0 us
  waiting for transfers between devices: 3.24 us -> 45.3 us
  Pallas kernels: 0 us -> 27 us
  matrix products: 21.9 us -> 0 us
  local copies, waits for them, and re-layouts: 19.6 us -> 1.8 us
  starting transfers between devices: 11 us -> 27.2 us
  other arithmetic: 5.54 us -> 0.95 us
    all_gather x2 -> x0, blocking collectives: 57.1 us -> none  [the longest x1 44.3 us: body(): piece_queries = lax.all_gather(queries, 'own', axis=0, tiled=True)]
    all_to_all x2, waiting for transfers between devices: 3.24 us -> 43.3 us  [exchange(): return lax.all_to_all(x, axes, split_axis=0, concat_axis=0, tiled=True)]
    all_to_all x1 -> x0, blocking collectives: 30.8 us -> none  [body(): lax.all_to_all(outgoing, ('grp', 'own'), split_axis=0, concat_axis=0, til...]
    pallas_call x0 -> x5, Pallas kernels: none -> 27 us  [the longest x1 10.8 us: score_labels(): pl.pallas_call(functools.partial(label_kernel, sources, capacity), in_spe...]
    dot_general x4 -> x0, matrix products: 21.9 us -> none  [the longest x1 10.1 us: owner_scores(): jnp.einsum('scmd,cld->scml', arrived, label_weights, preferred_element_ty...]
    psum x1 -> x0, blocking collectives: 13.5 us -> none  [body(): totals, picks = lax.psum((totals * jnp.exp(maxima - top_max), picks), 'own')]
    pmax x1 -> x0, blocking collectives: 12 us -> none  [body(): top_max = lax.pmax(maxima, 'own')]
    ppermute x0 -> x8, starting transfers between devices: none -> 11.1 us  [the longest x6 8.79 us: shift(): lax.ppermute(x, 'own', [(i, (i + by) % owners) for i in range(owners)])]
  transfers between devices with their start and end apart: 2 -> 10, of which waited for: 1 -> 4; matrix products, arithmetic and copies ran while one was open for 14% -> 1% of each run, Pallas kernels for 0% -> 22%
where the time goes in v1:
time: 103 us
  waiting for transfers between devices  45.3 us (44%)
  starting transfers between devices  27.2 us (26%)
  Pallas kernels  27 us (26%)
  local copies, waits for them, and re-layouts  1.8 us (2%)
    all_to_all x2, waiting for transfers between devices, exchange(): return lax.all_to_all(x, axes, split_axis=0, concat_axis=0, tiled=True)  43.3 us
    all_to_all x2, starting transfers between devices, exchange(): return lax.all_to_all(x, axes, split_axis=0, concat_axis=0, tiled=True)  16.1 us
    pallas_call x1, Pallas kernels, score_labels(): pl.pallas_call(functools.partial(label_kernel, sources, capacity), in_spe...  10.8 us
    ppermute x6, starting transfers between devices, shift(): lax.ppermute(x, 'own', [(i, (i + by) % owners) for i in range(owners)])  8.79 us
    pallas_call x1, Pallas kernels, score_centroids(): pl.pallas_call(functools.partial(centroid_kernel, spacing), in_specs=[who...  7.34 us
    pallas_call x1, Pallas kernels, join(): pl.pallas_call(functools.partial(join_kernel, capacity, columns), in_spec...  4.31 us
    pallas_call x1, Pallas kernels, route(): pl.pallas_call(functools.partial(route_kernel, clusters, capacity), out_s...  2.83 us
    ppermute x2, starting transfers between devices, swap(): lax.ppermute(x, 'own', [(i, i ^ 1) for i in range(lax.axis_size('own'))])  2.29 us
  transfers between devices with their start and end apart: 10, of which 4 were waited for; matrix products, arithmetic and copies ran while one was open for 1% of the time, Pallas kernels for 22%

profile of v1, /device:TPU:1, one launch (start us, length us, event | category | flops | bytes accessed | tf_op | source)
XLA Modules:
  0.0 102.6 jit_solution(9565416337098036117)
XLA Ops:
  0.0 2.0 %collective-permute-start = (bf16[32,1024]{1,0:T(8,128)(2,1)}, bf16[32,1024]{1,0:T(8,128)(2,1)S(1)}, u32[]{:S(2)}, u32[]{:S(2)}) collective-permute-start(bf16[32,1024]{1,0:T(8,128)(2,1)} %refs_0_), channel_id=1, source_target_pairs={{0,2},{1,3},{2,4},{3,5},{4,6},{5,7},{6,0},{7,1},{8,10},{9,11},{10,... | collective-permute-start | bytes 196616 | tf_op jit(solution)/shard_map/ppermute | solution.py:338
  2.0 2.5 %collective-permute-start.1 = (bf16[32,1024]{1,0:T(8,128)(2,1)}, bf16[32,1024]{1,0:T(8,128)(2,1)S(1)}, u32[]{:S(2)}, u32[]{:S(2)}) collective-permute-start(bf16[32,1024]{1,0:T(8,128)(2,1)} %refs_0_), channel_id=1, source_target_pairs={{0,4},{1,5},{2,6},{3,7},{4,0},{5,1},{6,2},{7,3},{8,12},{9,13},{10,... | collective-permute-start | bytes 196616 | tf_op jit(solution)/shard_map/ppermute | solution.py:338
  4.5 1.2 %collective-permute-start.2 = (bf16[32,1024]{1,0:T(8,128)(2,1)}, bf16[32,1024]{1,0:T(8,128)(2,1)S(1)}, u32[]{:S(2)}, u32[]{:S(2)}) collective-permute-start(bf16[32,1024]{1,0:T(8,128)(2,1)} %refs_0_), channel_id=1, source_target_pairs={{0,6},{1,7},{2,0},{3,1},{4,2},{5,3},{6,4},{7,5},{8,14},{9,15},{10,... | collective-permute-start | bytes 196616 | tf_op jit(solution)/shard_map/ppermute | solution.py:338
  5.6 2.8 %route.1 = (bf16[4096,128]{1,0:T(8,128)(2,1)}, s32[8,32]{1,0:T(8,128)}) custom-call(bf16[32,1024]{1,0:T(8,128)(2,1)} %refs_0_, s32[8,32]{1,0:T(8,128)} %bitcast.14), custom_call_target="tpu_custom_call" | custom-call | tf_op jit(solution)/shard_map/route/pallas_call | solution.py:55
  8.5 0.0 collective-permute-done.refs_1_
  8.5 0.0 copy-start.2
  8.5 0.0 collective-permute-done.1.refs_2_
  8.5 0.0 copy-start.3
  8.5 0.0 collective-permute-done.2.refs_3_
  8.5 0.0 copy-start.4
  8.6 11.3 %all-to-all-start = ((bf16[128,32,128]{2,1,0:T(8,128)(2,1)}), bf16[128,32,128]{2,1,0:T(8,128)(2,1)S(1)}, u32[]{:S(2)}, u32[]{:S(2)}) async-start(bf16[128,32,128]{2,1,0:T(8,128)(2,1)} %bitcast.13), calls=%async_computation | async-start | bytes 2097152 | tf_op jit(solution)/shard_map/all_to_all | solution.py:333
  19.8 0.9 pad_maximum_fusion
  20.7 1.1 %collective-permute-start.3 = (bf16[128,1024]{1,0:T(8,128)(2,1)S(1)}, bf16[128,1024]{1,0:T(8,128)(2,1)S(1)}, u32[]{:S(2)}, u32[]{:S(2)}) collective-permute-start(bf16[128,1024]{1,0:T(8,128)(2,1)S(1)} %pad_maximum_fusion), channel_id=1, source_target_pairs={{0,1},{1,0},{2,3},{3,2},{4,5},{5,4},{6,7},{7,6},{8,9},{9,8},{10,11... | collective-permute-start | bytes 786440 | tf_op jit(solution)/shard_map/ppermute | solution.py:342
  21.8 1.2 %collective-permute-done.3.refs_4_ = bf16[128,1024]{1,0:T(8,128)(2,1)S(1)} collective-permute-done((bf16[128,1024]{1,0:T(8,128)(2,1)S(1)}, bf16[128,1024]{1,0:T(8,128)(2,1)S(1)}, u32[]{:S(2)}, u32[]{:S(2)}) %collective-permute-start.3) | collective-permute-done | bytes 262176 | tf_op jit(solution)/shard_map/ppermute | solution.py:342
  23.0 0.0 copy-done.2
  23.0 0.0 copy-done.3
  23.0 0.0 copy-done.4
  23.0 0.0 copy-start.5
  23.0 0.7 copy-done.5
  23.7 7.3 %score_centroids.1 = (f32[64,128]{1,0:T(8,128)}, f32[64,128]{1,0:T(8,128)}, f32[64,128]{1,0:T(8,128)}, f32[64,128]{1,0:T(8,128)}) custom-call(bf16[32,1024]{1,0:T(8,128)(2,1)} %refs_0_, bf16[32,1024]{1,0:T(8,128)(2,1)} %copy-done.2, bf16[32,1024]{1,0:T(8,128)(2,1)} %copy-done.3, bf16[32,1024]{1,0:T(8,128)(2,1)} %copy-done.4, bf16[128,1024]{1,0:T(8,128)(2,1)} %copy-done.5, ...), custom_call_target="tpu_custom_call" | custom-call | flops 2147483648 | bytes 8388608 | tf_op jit(solution)/shard_map/score_centroids/pallas_call | solution.py:220
  31.1 2.0 %collective-permute-start.4 = (f32[64,128]{1,0:T(8,128)}, f32[64,128]{1,0:T(8,128)S(1)}, u32[]{:S(2)}, u32[]{:S(2)}) collective-permute-start(f32[64,128]{1,0:T(8,128)} %get-tuple-element.31), channel_id=1, source_target_pairs={{0,6},{1,7},{2,0},{3,1},{4,2},{5,3},{6,4},{7,5},{8,14},{9,15},{10,... | collective-permute-start | bytes 98312 | tf_op jit(solution)/shard_map/ppermute | solution.py:338
  33.0 0.6 collective-permute-start.5
  33.6 0.6 collective-permute-start.6
  34.2 5.0 %all-to-all-done = bf16[128,32,128]{2,1,0:T(8,128)(2,1)S(1)} async-done(((bf16[128,32,128]{2,1,0:T(8,128)(2,1)}), bf16[128,32,128]{2,1,0:T(8,128)(2,1)S(1)}, u32[]{:S(2)}, u32[]{:S(2)}) %all-to-all-start) | async-done | bytes 1048608 | tf_op jit(solution)/shard_map/all_to_all | solution.py:333
  39.2 0.0 copy-start.1
  39.2 1.0 copy-done.1
  40.1 10.8 %score_labels.1 = bf16[12544,128]{1,0:T(8,128)(2,1)} custom-call(bf16[4096,128]{1,0:T(8,128)(2,1)} %bitcast.12, bf16[2,3072,1024]{2,1,0:T(8,128)(2,1)} %weights_ref.1), custom_call_target="tpu_custom_call" | custom-call | flops 3221225472 | bytes 12582912 | tf_op jit(solution)/shard_map/score_labels/pallas_call | solution.py:154
  51.0 0.0 collective-permute-done.4
  51.0 0.0 collective-permute-done.5
  51.0 0.0 collective-permute-done.6
  51.0 0.0 copy-start.7
  51.0 0.0 copy-start.6
  51.1 0.0 copy-start
  51.1 4.8 %all-to-all-start.1 = ((bf16[128,49,2,128]{3,2,1,0:T(2,128)(2,1)}), bf16[128,49,2,128]{3,2,1,0:T(2,128)(2,1)S(1)}, u32[]{:S(2)}, u32[]{:S(2)}) async-start(bf16[128,49,2,128]{3,2,1,0:T(2,128)(2,1)} %bitcast.11), calls=%async_computation.1 | async-start | bytes 6422528 | tf_op jit(solution)/shard_map/all_to_all | solution.py:333
  55.9 0.0 copy-done.7
  55.9 0.1 copy.5.ids_ref
  56.0 0.0 copy-done.6
  56.0 1.1 %collective-permute-start.7 = (f32[128,128]{1,0:T(8,128)S(1)}, f32[128,128]{1,0:T(8,128)S(1)}, u32[]{:S(2)}, u32[]{:S(2)}) collective-permute-start(f32[128,128]{1,0:T(8,128)S(1)} %pad_maximum_fusion.1), channel_id=1, source_target_pairs={{0,1},{1,0},{2,3},{3,2},{4,5},{5,4},{6,7},{7,6},{8,9},{9,8},{10,11... | collective-permute-start | bytes 196616 | tf_op jit(solution)/shard_map/ppermute | solution.py:342
  57.2 0.1 pad_add_fusion.owner_ref
  57.3 0.8 collective-permute-done.7.refs_4_
  58.1 1.6 %priors.1.prior_ref = f32[8,32,128]{2,1,0:T(8,128)S(1)} custom-call(s32[8]{0:T(128)S(1)} %pad_add_fusion.owner_ref, s32[32,8]{1,0:T(8,128)S(1)} %copy.5.ids_ref, f32[32,128]{1,0:T(8,128)S(1)} %get-tuple-element.40.refs_0_, f32[32,128]{1,0:T(8,128)S(1)} %get-tuple-element.47.refs_1_, f32[32,128]{1,0:T(8,128)S(1)} %get-tuple-element.44.refs_2_, ...), custom_call_target="tpu_custom_call" | custom-call | tf_op jit(solution)/shard_map/priors/pallas_call | solution.py:261
  59.7 38.4 %all-to-all-done.1 = bf16[128,49,2,128]{3,2,1,0:T(2,128)(2,1)S(1)} async-done(((bf16[128,49,2,128]{3,2,1,0:T(2,128)(2,1)}), bf16[128,49,2,128]{3,2,1,0:T(2,128)(2,1)S(1)}, u32[]{:S(2)}, u32[]{:S(2)}) %all-to-all-start.1) | async-done | bytes 3211296 | tf_op jit(solution)/shard_map/all_to_all | solution.py:333
  98.1 0.0 copy-done
  98.1 4.3 %join.1 = f32[6144,128]{1,0:T(8,128)} custom-call(s32[8,32]{1,0:T(8,128)S(1)} %copy-done, f32[8,32,128]{2,1,0:T(8,128)S(1)} %priors.1.prior_ref, bf16[12544,128]{1,0:T(8,128)(2,1)S(1)} %bitcast.10), custom_call_target="tpu_custom_call" | custom-call | tf_op jit(solution)/shard_map/join/pallas_call | solution.py:315
  (4 shorter events, 0.0 us)
Async XLA Ops:
  0.0 8.5 %collective-permute-start = (bf16[32,1024]{1,0:T(8,128)(2,1)}, bf16[32,1024]{1,0:T(8,128)(2,1)S(1)}, u32[]{:S(2)}, u32[]{:S(2)}) collective-permute-start(bf16[32,1024]{1,0:T(8,128)(2,1)} %refs_0_), channel_id=1, source_target_pairs={{0,2},{1,3},{2,4},{3,5},{4,6},{5,7},{6,0},{7,1},{8,10},{9,11},{10,... | collective-permute-start | bytes 196616 | tf_op jit(solution)/shard_map/ppermute | solution.py:338
  2.0 6.5 %collective-permute-start.1 = (bf16[32,1024]{1,0:T(8,128)(2,1)}, bf16[32,1024]{1,0:T(8,128)(2,1)S(1)}, u32[]{:S(2)}, u32[]{:S(2)}) collective-permute-start(bf16[32,1024]{1,0:T(8,128)(2,1)} %refs_0_), channel_id=1, source_target_pairs={{0,4},{1,5},{2,6},{3,7},{4,0},{5,1},{6,2},{7,3},{8,12},{9,13},{10,... | collective-permute-start | bytes 196616 | tf_op jit(solution)/shard_map/ppermute | solution.py:338
  4.5 4.0 %collective-permute-start.2 = (bf16[32,1024]{1,0:T(8,128)(2,1)}, bf16[32,1024]{1,0:T(8,128)(2,1)S(1)}, u32[]{:S(2)}, u32[]{:S(2)}) collective-permute-start(bf16[32,1024]{1,0:T(8,128)(2,1)} %refs_0_), channel_id=1, source_target_pairs={{0,6},{1,7},{2,0},{3,1},{4,2},{5,3},{6,4},{7,5},{8,14},{9,15},{10,... | collective-permute-start | bytes 196616 | tf_op jit(solution)/shard_map/ppermute | solution.py:338
  8.5 14.5 %copy-start.2 = (bf16[32,1024]{1,0:T(8,128)(2,1)}, bf16[32,1024]{1,0:T(8,128)(2,1)S(1)}, u32[]{:S(2)}) copy-start(bf16[32,1024]{1,0:T(8,128)(2,1)S(1)} %collective-permute-done.refs_1_) | copy-start | bytes 196612
  8.5 14.5 %copy-start.3 = (bf16[32,1024]{1,0:T(8,128)(2,1)}, bf16[32,1024]{1,0:T(8,128)(2,1)S(1)}, u32[]{:S(2)}) copy-start(bf16[32,1024]{1,0:T(8,128)(2,1)S(1)} %collective-permute-done.1.refs_2_) | copy-start | bytes 196612
  8.5 14.5 %copy-start.4 = (bf16[32,1024]{1,0:T(8,128)(2,1)}, bf16[32,1024]{1,0:T(8,128)(2,1)S(1)}, u32[]{:S(2)}) copy-start(bf16[32,1024]{1,0:T(8,128)(2,1)S(1)} %collective-permute-done.2.refs_3_) | copy-start | bytes 196612
  8.6 30.6 %all-to-all-start = ((bf16[128,32,128]{2,1,0:T(8,128)(2,1)}), bf16[128,32,128]{2,1,0:T(8,128)(2,1)S(1)}, u32[]{:S(2)}, u32[]{:S(2)}) async-start(bf16[128,32,128]{2,1,0:T(8,128)(2,1)} %bitcast.13), calls=%async_computation | async-start | bytes 2097152 | tf_op jit(solution)/shard_map/all_to_all | solution.py:333
  20.7 2.3 %collective-permute-start.3 = (bf16[128,1024]{1,0:T(8,128)(2,1)S(1)}, bf16[128,1024]{1,0:T(8,128)(2,1)S(1)}, u32[]{:S(2)}, u32[]{:S(2)}) collective-permute-start(bf16[128,1024]{1,0:T(8,128)(2,1)S(1)} %pad_maximum_fusion), channel_id=1, source_target_pairs={{0,1},{1,0},{2,3},{3,2},{4,5},{5,4},{6,7},{7,6},{8,9},{9,8},{10,11... | collective-permute-start | bytes 786440 | tf_op jit(solution)/shard_map/ppermute | solution.py:342
  23.0 0.7 copy-start.5
  31.1 19.9 %collective-permute-start.4 = (f32[64,128]{1,0:T(8,128)}, f32[64,128]{1,0:T(8,128)S(1)}, u32[]{:S(2)}, u32[]{:S(2)}) collective-permute-start(f32[64,128]{1,0:T(8,128)} %get-tuple-element.31), channel_id=1, source_target_pairs={{0,6},{1,7},{2,0},{3,1},{4,2},{5,3},{6,4},{7,5},{8,14},{9,15},{10,... | collective-permute-start | bytes 98312 | tf_op jit(solution)/shard_map/ppermute | solution.py:338
  33.0 18.0 %collective-permute-start.5 = (f32[64,128]{1,0:T(8,128)}, f32[64,128]{1,0:T(8,128)S(1)}, u32[]{:S(2)}, u32[]{:S(2)}) collective-permute-start(f32[64,128]{1,0:T(8,128)} %get-tuple-element.32), channel_id=1, source_target_pairs={{0,4},{1,5},{2,6},{3,7},{4,0},{5,1},{6,2},{7,3},{8,12},{9,13},{10,... | collective-permute-start | bytes 98312 | tf_op jit(solution)/shard_map/ppermute | solution.py:338
  33.6 17.4 %collective-permute-start.6 = (f32[64,128]{1,0:T(8,128)}, f32[64,128]{1,0:T(8,128)S(1)}, u32[]{:S(2)}, u32[]{:S(2)}) collective-permute-start(f32[64,128]{1,0:T(8,128)} %get-tuple-element.33), channel_id=1, source_target_pairs={{0,2},{1,3},{2,4},{3,5},{4,6},{5,7},{6,0},{7,1},{8,10},{9,11},{10,... | collective-permute-start | bytes 98312 | tf_op jit(solution)/shard_map/ppermute | solution.py:338
  39.2 1.0 copy-start.1
  51.0 4.9 %copy-start.7 = (s32[32,8]{0,1:T(8,128)S(1)}, s32[32,8]{0,1:T(8,128)}, u32[]{:S(2)}) copy-start(s32[32,8]{0,1:T(8,128)} %param.6) | copy-start | bytes 3076
  51.0 5.0 %copy-start.6 = (f32[64,128]{1,0:T(8,128)S(1)}, f32[64,128]{1,0:T(8,128)}, u32[]{:S(2)}) copy-start(f32[64,128]{1,0:T(8,128)} %get-tuple-element.34) | copy-start | bytes 98308
  51.1 47.1 %copy-start = (s32[8,32]{1,0:T(8,128)S(1)}, s32[8,32]{1,0:T(8,128)}, u32[]{:S(2)}) copy-start(s32[8,32]{1,0:T(8,128)} %get-tuple-element.22.slot_ref) | copy-start | bytes 3076
  51.1 47.0 %all-to-all-start.1 = ((bf16[128,49,2,128]{3,2,1,0:T(2,128)(2,1)}), bf16[128,49,2,128]{3,2,1,0:T(2,128)(2,1)S(1)}, u32[]{:S(2)}, u32[]{:S(2)}) async-start(bf16[128,49,2,128]{3,2,1,0:T(2,128)(2,1)} %bitcast.11), calls=%async_computation.1 | async-start | bytes 6422528 | tf_op jit(solution)/shard_map/all_to_all | solution.py:333
  56.0 2.0 %collective-permute-start.7 = (f32[128,128]{1,0:T(8,128)S(1)}, f32[128,128]{1,0:T(8,128)S(1)}, u32[]{:S(2)}, u32[]{:S(2)}) collective-permute-start(f32[128,128]{1,0:T(8,128)S(1)} %pad_maximum_fusion.1), channel_id=1, source_target_pairs={{0,1},{1,0},{2,3},{3,2},{4,5},{5,4},{6,7},{7,6},{8,9},{9,8},{10,11... | collective-permute-start | bytes 196616 | tf_op jit(solution)/shard_map/ppermute | solution.py:342

commit v2 on v1

--- a/solution.py
+++ b/solution.py
@@ -12,7 +12,7 @@
 MIB = 1 << 20
 
 
-def route_kernel(clusters, capacity, queries_hbm, ids_hbm, out_ref, slot_ref, queries_ref, ids_ref, stage, sems):
+def route_kernel(clusters, capacity, held, columns, queries_hbm, ids_hbm, out_ref, row_ref, total_ref, queries_ref, ids_ref, stage, sems):
     copies = [
         pltpu.make_async_copy(ids_hbm, ids_ref, sems.at[0]),
         pltpu.make_async_copy(queries_hbm, queries_ref, sems.at[1]),
@@ -46,16 +46,21 @@
     rank = jnp.concatenate(
         [jnp.sum(jnp.where(n, before, 0.0), axis=0, keepdims=True) for n in named], axis=0
     )
-    slot_ref[...] = ids_ref[...] * capacity + rank.astype(jnp.int32)
-
-
-def route(queries, ids, clusters, capacity):
+    places = held * capacity
+    source = ids_ref[...] // held
+    place = ids_ref[...] % held * capacity + rank.astype(jnp.int32)
+    row_ref[...] = source * (places * columns + 2) + place * columns
+    total_ref[...] = place * (clusters // held) + source
+
+
+def route(queries, ids, clusters, capacity, held, columns):
     rows, width = queries.shape
     total = clusters * capacity * width // LANES
     return pl.pallas_call(
-        functools.partial(route_kernel, clusters, capacity),
+        functools.partial(route_kernel, clusters, capacity, held, columns),
         out_shape=(
             jax.ShapeDtypeStruct((total, LANES), BF16),
+            jax.ShapeDtypeStruct(ids.shape, jnp.int32),
             jax.ShapeDtypeStruct(ids.shape, jnp.int32),
         ),
         in_specs=[pl.BlockSpec(memory_space=pltpu.HBM)] * 2,
@@ -70,22 +75,26 @@
     )(queries, ids)
 
 
-def label_kernel(sources, capacity, arrived_ref, weights_ref, out_ref, spread, x, w, logits, stage, pack, sems, out_sems):
+def label_kernel(
+    sources, capacity, arrived_ref, weights_ref, out_ref, spread, x, w, peak, mass, stage, pack, sems, out_sems
+):
     held, labels, width = weights_ref.shape
     tiles, columns = width // LANES, labels // LANES
     rows = stage.shape[0] // sources
-    blocks = w.shape[1]
-    block = labels // blocks
-    here = block // LANES
     parts = out_sems.shape[0]
     count = sources // parts
-
-    copies = {
-        (c, n): pltpu.make_async_copy(weights_ref.at[c, pl.ds(n * block, block)], w.at[c, n], sems.at[c, n])
-        for c in range(held)
-        for n in range(blocks)
-    }
-    for copy in copies.values():
+    places = held * capacity
+    block = 512
+    here = block // LANES
+
+    size = labels // sems.shape[1]
+    pieces = []
+    for c in range(held):
+        for i in range(sems.shape[1]):
+            part = pl.ds(i * size, size)
+            pieces.append((c, i * size, pltpu.make_async_copy(weights_ref.at[c, part], w.at[c, part], sems.at[c, i])))
+    ahead = 2
+    for *_, copy in pieces[:ahead]:
         copy.start()
     spread[...] = arrived_ref[...].astype(F32)
 
@@ -96,47 +105,50 @@
                     pl.ds((c * capacity + m) * tiles + k, sources, stride=held * capacity * tiles), :
                 ].astype(BF16)
 
-    def product(c, n):
-        copies[c, n].wait()
-        scores = lax.dot_general(x[c], w[c, n], (((1,), (1,)), ((), ())), preferred_element_type=F32)
-        logits[c, :, n * block : (n + 1) * block] = scores
+    def product(c, first):
+        scores = lax.dot_general(
+            x[c], w[c, first : first + block, :], (((1,), (1,)), ((), ())), preferred_element_type=F32
+        )
         for m in range(capacity):
             for j in range(here):
-                stage[pl.ds((c * capacity + m) * columns + n * here + j, sources, stride=rows), :] = scores[
+                stage[pl.ds((c * capacity + m) * columns + first // LANES + j, sources, stride=rows), :] = scores[
                     m * sources : (m + 1) * sources, j * LANES : (j + 1) * LANES
                 ]
-
-    def total(c, m, p):
-        scores = logits[c, m * sources + p * count : m * sources + (p + 1) * count, :]
-        largest = jnp.max(scores, axis=1, keepdims=True)
-        return largest + jnp.log(jnp.sum(jnp.exp(scores - largest), axis=1, keepdims=True))
-
-    totals = {}
-    places = held * capacity
+        cuts = [scores[:, j * LANES : (j + 1) * LANES] for j in range(here)]
+        largest = functools.reduce(jnp.maximum, cuts)
+        if first > 0:
+            before = peak[c]
+            largest = jnp.maximum(largest, before)
+        summed = sum(jnp.exp(cut - largest) for cut in cuts)
+        if first > 0:
+            summed = summed + mass[c] * jnp.exp(before - largest)
+        peak[c] = largest
+        mass[c] = summed
+
+    for i, (c, first, copy) in enumerate(pieces):
+        if first == 0:
+            gather(c)
+        copy.wait()
+        for *_, later in pieces[i + ahead : i + ahead + 1]:
+            later.start()
+        for n in range(size // block):
+            product(c, first + n * block)
+
+    lane = lax.broadcasted_iota(jnp.int32, (sources, LANES), 1)
+    packed = jnp.zeros((sources, LANES), F32)
     for c in range(held):
-        gather(c)
-        for n in range(blocks):
-            product(c, n)
-            if c > 0:
-                for p in range(n * parts // blocks, (n + 1) * parts // blocks):
-                    for m in range(capacity):
-                        totals[c - 1, m, p] = total(c - 1, m, p)
-
-    lane = lax.broadcasted_iota(jnp.int32, (count, LANES), 1)
+        largest = jnp.max(peak[c], axis=1, keepdims=True)
+        total = largest + jnp.log(jnp.sum(mass[c] * jnp.exp(peak[c] - largest), axis=1, keepdims=True))
+        for m in range(capacity):
+            rest = total[m * sources : (m + 1) * sources]
+            for t in range(3):
+                term = rest.astype(BF16).astype(F32)
+                packed = jnp.where(lane == t * places + c * capacity + m, term, packed)
+                rest = rest - term
+    stage[pl.ds(places * columns, sources, stride=rows), :] = packed
+    stage[pl.ds(places * columns + 1, sources, stride=rows), :] = jnp.zeros_like(packed)
     outs = []
     for p in range(parts):
-        for m in range(capacity):
-            totals[held - 1, m, p] = total(held - 1, m, p)
-        packed = jnp.zeros((count, LANES), F32)
-        for c in range(held):
-            for m in range(capacity):
-                rest = totals[c, m, p]
-                for t in range(3):
-                    term = rest.astype(BF16).astype(F32)
-                    packed = jnp.where(lane == t * places + c * capacity + m, term, packed)
-                    rest = rest - term
-        stage[pl.ds(p * count * rows + places * columns, count, stride=rows), :] = packed
-        stage[pl.ds(p * count * rows + places * columns + 1, count, stride=rows), :] = jnp.zeros_like(packed)
         span = pl.ds(p * count * rows, count * rows)
         pack[span, :] = stage[span, :].astype(BF16)
         out = pltpu.make_async_copy(pack.at[span], out_ref.at[span], out_sems.at[p])
@@ -149,7 +161,6 @@
 def score_labels(arrived, weights, sources, capacity):
     held, labels, width = weights.shape
     slots = sources * capacity
-    blocks = 2
     rows = held * capacity * labels // LANES + 2
     return pl.pallas_call(
         functools.partial(label_kernel, sources, capacity),
@@ -159,14 +170,15 @@
         scratch_shapes=[
             pltpu.VMEM(arrived.shape, F32),
             pltpu.VMEM((held, slots, width), BF16),
-            pltpu.VMEM((held, blocks, labels // blocks, width), BF16),
-            pltpu.VMEM((held, slots, labels), F32),
+            pltpu.VMEM(weights.shape, BF16),
+            pltpu.VMEM((held, slots, LANES), F32),
+            pltpu.VMEM((held, slots, LANES), F32),
             pltpu.VMEM((sources * rows, LANES), F32),
             pltpu.VMEM((sources * rows, LANES), BF16),
-            pltpu.SemaphoreType.DMA((held, blocks)),
+            pltpu.SemaphoreType.DMA((held, 2)),
             pltpu.SemaphoreType.DMA((4,)),
         ],
-        compiler_params=pltpu.CompilerParams(vmem_limit_bytes=54 * MIB),
+        compiler_params=pltpu.CompilerParams(vmem_limit_bytes=50 * MIB),
         cost_estimate=pl.CostEstimate(
             flops=2 * held * slots * labels * width,
             bytes_accessed=2 * held * labels * width,
@@ -268,64 +280,56 @@
     )(owners, ids, *shares)
 
 
-def join_kernel(capacity, columns, slot_ref, prior_ref, scores_ref, out_ref, total_b, wide, ready, sems):
+def join_kernel(places, columns, row_ref, place_ref, prior_ref, scores_ref, out_ref, totals, wide, ready, sems):
     beam, queries, _ = prior_ref.shape
-    per_owner, sources, _ = total_b.shape
-    rows = scores_ref.shape[0] // sources
+    rows = places * columns + 2
+    sources = scores_ref.shape[0] // rows
     spans = 8
     span = scores_ref.shape[0] // spans
     for i in range(spans):
         wide[i * span : (i + 1) * span, :] = scores_ref[i * span : (i + 1) * span, :].astype(F32)
-    terms = wide[pl.ds(per_owner * columns, sources, stride=rows), :]
-    for j in range(per_owner):
-        total = sum(terms[:, t * per_owner + j : t * per_owner + j + 1] for t in range(3))
-        total_b[j] = jnp.broadcast_to(total, (sources, LANES))
+    terms = wide[pl.ds(places * columns, sources, stride=rows), :]
+    for j in range(places):
+        total = sum(terms[:, t * places + j : t * places + j + 1] for t in range(3))
+        totals[j * sources : (j + 1) * sources, :] = jnp.broadcast_to(total, (sources, LANES))
 
     parts = sems.shape[0]
     block = queries // parts
 
     def copy(g):
-        here = pl.ds(pl.multiple_of(g * block * beam * columns, 8), block * beam * columns)
+        here = pl.ds(g * block * beam * columns, block * beam * columns)
         return pltpu.make_async_copy(ready.at[here], out_ref.at[here], sems.at[g])
 
-    @pl.loop(0, parts)
-    def _(g):
-        for i in range(block):
-            q = g * block + i
+    for g in range(parts):
+        for q in range(g * block, (g + 1) * block):
             for s in range(beam):
-                slot = slot_ref[s, q]
-                source = slot // per_owner
-                place = slot % per_owner
-                row = wide[pl.ds(source * rows + place * columns, columns), :]
-                shift = prior_ref[s, pl.ds(q, 1), :] - total_b[place, pl.ds(source, 1), :]
+                row = wide[pl.ds(row_ref[s, q], columns), :]
+                shift = prior_ref[s, q : q + 1, :] - totals[pl.ds(place_ref[s, q], 1), :]
                 ready[pl.ds(q * beam * columns + s, columns, stride=beam), :] = row + shift
         copy(g).start()
-
-    @pl.loop(0, parts)
-    def _(g):
+    for g in range(parts):
         copy(g).wait()
 
 
-def join(slots, prior, scores, capacity, held, labels):
-    beam, queries = slots.shape
+def join(row_of, place_of, prior, scores, places, labels):
+    beam, queries = row_of.shape
     columns = labels // LANES
-    places = held * capacity
     sources = scores.shape[0] // (places * columns + 2)
     whole = pl.BlockSpec(memory_space=pltpu.VMEM)
     out = pl.pallas_call(
-        functools.partial(join_kernel, capacity, columns),
-        in_specs=[pl.BlockSpec(memory_space=pltpu.SMEM)] + [whole] * 2,
+        functools.partial(join_kernel, places, columns),
+        in_specs=[pl.BlockSpec(memory_space=pltpu.SMEM)] * 2 + [whole] * 2,
         out_specs=pl.BlockSpec(memory_space=pltpu.HBM),
         out_shape=jax.ShapeDtypeStruct((queries * beam * columns, LANES), F32),
         scratch_shapes=[
-            pltpu.VMEM((places, sources, LANES), F32),
+            pltpu.VMEM((places * sources, LANES), F32),
             pltpu.VMEM(scores.shape, F32),
             pltpu.VMEM((queries * beam * columns, LANES), F32),
             pltpu.SemaphoreType.DMA((8,)),
         ],
         compiler_params=pltpu.CompilerParams(vmem_limit_bytes=24 * MIB),
         name="join",
-    )(slots, prior, scores)
+    )(row_of, place_of, prior, scores)
     return out.reshape(queries, columns, beam, LANES).transpose(0, 2, 1, 3).reshape(queries, beam, labels)
 
 
@@ -356,7 +360,7 @@
     hops = range(2, owners, 2)
 
     mine = [queries] + [shift(queries, by) for by in hops]
-    outgoing, slots = route(queries, cluster_ids.T, clusters, capacity)
+    outgoing, row_of, place_of = route(queries, cluster_ids.T, clusters, capacity, held, labels // LANES)
     outgoing, *mine = lax.optimization_barrier((outgoing, *mine))
     arrived = exchange(outgoing, everyone)
 
@@ -375,7 +379,7 @@
     steps = jnp.arange(0, owners, 2, dtype=jnp.int32)
     shard = jnp.concatenate([(here + steps) % owners, ((here ^ 1) + steps) % owners]).astype(jnp.int32)
     prior = priors(shard, cluster_ids, [share[:rows] for share in back] + [mate], heads)
-    return join(slots, prior, scores_home, capacity, held, labels)
+    return join(row_of, place_of, prior, scores_home, held * capacity, labels)
 
 
 def solution(mesh):

time: 103 us -> 99.4 us (0.965)
  Pallas kernels: 27 us -> 24.3 us
    pallas_call x1, Pallas kernels: 10.8 us -> 9.43 us  [score_labels(): pl.pallas_call(functools.partial(label_kernel, sources, capacity), in_spe...]
    pallas_call x2, Pallas kernels: 7.15 us -> 5.89 us  [the longest x1 3.05 us: join(): pl.pallas_call(functools.partial(join_kernel, places, columns), in_specs=...]
  transfers between devices with their start and end apart: 10 -> 10, of which waited for: 4 -> 4; matrix products, arithmetic and copies ran while one was open for 1% -> 1% of each run, Pallas kernels for 22% -> 21%
where the time goes in v2:
time: 99.4 us; the launch traced here: 99 us
  waiting for transfers between devices  45.3 us (46%)
  starting transfers between devices  27.2 us (27%)
  Pallas kernels  24.3 us (24%)
    all_to_all x2, waiting for transfers between devices, exchange(): return lax.all_to_all(x, axes, split_axis=0, concat_axis=0, tiled=True)  43.3 us
    all_to_all x2, starting transfers between devices, exchange(): return lax.all_to_all(x, axes, split_axis=0, concat_axis=0, tiled=True)  16.1 us
    pallas_call x1, Pallas kernels, score_labels(): pl.pallas_call(functools.partial(label_kernel, sources, capacity), in_spe...  9.43 us
    ppermute x6, starting transfers between devices, shift(): lax.ppermute(x, 'own', [(i, (i + by) % owners) for i in range(owners)])  8.79 us
    pallas_call x1, Pallas kernels, score_centroids(): pl.pallas_call(functools.partial(centroid_kernel, spacing), in_specs=[who...  7.34 us
    pallas_call x1, Pallas kernels, join(): pl.pallas_call(functools.partial(join_kernel, places, columns), in_specs=...  3.05 us
    pallas_call x1, Pallas kernels, route(): pl.pallas_call(functools.partial(route_kernel, clusters, capacity, held,...  2.84 us
    ppermute x2, starting transfers between devices, swap(): lax.ppermute(x, 'own', [(i, i ^ 1) for i in range(lax.axis_size('own'))])  2.29 us
  transfers between devices with their start and end apart: 10, of which 4 were waited for; matrix products, arithmetic and copies ran while one was open for 1% of the time, Pallas kernels for 21%

profile of v2, /device:TPU:1, one launch (start us, length us, event | category | flops | bytes accessed | tf_op | source)
XLA Modules:
  0.0 99.0 jit_solution(14285416897556724237)
XLA Ops:
  0.0 2.0 %collective-permute-start = (bf16[32,1024]{1,0:T(8,128)(2,1)}, bf16[32,1024]{1,0:T(8,128)(2,1)S(1)}, u32[]{:S(2)}, u32[]{:S(2)}) collective-permute-start(bf16[32,1024]{1,0:T(8,128)(2,1)} %refs_0_), channel_id=1, source_target_pairs={{0,2},{1,3},{2,4},{3,5},{4,6},{5,7},{6,0},{7,1},{8,10},{9,11},{10,... | collective-permute-start | bytes 196616 | tf_op jit(solution)/shard_map/ppermute | solution.py:342
  2.0 2.5 %collective-permute-start.1 = (bf16[32,1024]{1,0:T(8,128)(2,1)}, bf16[32,1024]{1,0:T(8,128)(2,1)S(1)}, u32[]{:S(2)}, u32[]{:S(2)}) collective-permute-start(bf16[32,1024]{1,0:T(8,128)(2,1)} %refs_0_), channel_id=1, source_target_pairs={{0,4},{1,5},{2,6},{3,7},{4,0},{5,1},{6,2},{7,3},{8,12},{9,13},{10,... | collective-permute-start | bytes 196616 | tf_op jit(solution)/shard_map/ppermute | solution.py:342
  4.5 1.2 %collective-permute-start.2 = (bf16[32,1024]{1,0:T(8,128)(2,1)}, bf16[32,1024]{1,0:T(8,128)(2,1)S(1)}, u32[]{:S(2)}, u32[]{:S(2)}) collective-permute-start(bf16[32,1024]{1,0:T(8,128)(2,1)} %refs_0_), channel_id=1, source_target_pairs={{0,6},{1,7},{2,0},{3,1},{4,2},{5,3},{6,4},{7,5},{8,14},{9,15},{10,... | collective-permute-start | bytes 196616 | tf_op jit(solution)/shard_map/ppermute | solution.py:342
  5.6 2.8 %route.1 = (bf16[4096,128]{1,0:T(8,128)(2,1)}, s32[8,32]{1,0:T(8,128)}, s32[8,32]{1,0:T(8,128)}) custom-call(bf16[32,1024]{1,0:T(8,128)(2,1)} %refs_0_, s32[8,32]{1,0:T(8,128)} %bitcast.14), custom_call_target="tpu_custom_call" | custom-call | tf_op jit(solution)/shard_map/route/pallas_call | solution.py:59
  8.5 0.0 collective-permute-done.refs_1_
  8.5 0.0 copy-start.2
  8.5 0.0 collective-permute-done.1.refs_2_
  8.5 0.0 copy-start.3
  8.5 0.0 collective-permute-done.2.refs_3_
  8.5 0.0 copy-start.4
  8.6 11.3 %all-to-all-start = ((bf16[128,32,128]{2,1,0:T(8,128)(2,1)}), bf16[128,32,128]{2,1,0:T(8,128)(2,1)S(1)}, u32[]{:S(2)}, u32[]{:S(2)}) async-start(bf16[128,32,128]{2,1,0:T(8,128)(2,1)} %bitcast.13), calls=%async_computation | async-start | bytes 2097152 | tf_op jit(solution)/shard_map/all_to_all | solution.py:337
  19.8 0.9 pad_maximum_fusion
  20.7 1.1 %collective-permute-start.3 = (bf16[128,1024]{1,0:T(8,128)(2,1)S(1)}, bf16[128,1024]{1,0:T(8,128)(2,1)S(1)}, u32[]{:S(2)}, u32[]{:S(2)}) collective-permute-start(bf16[128,1024]{1,0:T(8,128)(2,1)S(1)} %pad_maximum_fusion), channel_id=1, source_target_pairs={{0,1},{1,0},{2,3},{3,2},{4,5},{5,4},{6,7},{7,6},{8,9},{9,8},{10,11... | collective-permute-start | bytes 786440 | tf_op jit(solution)/shard_map/ppermute | solution.py:346
  21.8 1.2 %collective-permute-done.3.refs_4_ = bf16[128,1024]{1,0:T(8,128)(2,1)S(1)} collective-permute-done((bf16[128,1024]{1,0:T(8,128)(2,1)S(1)}, bf16[128,1024]{1,0:T(8,128)(2,1)S(1)}, u32[]{:S(2)}, u32[]{:S(2)}) %collective-permute-start.3) | collective-permute-done | bytes 262176 | tf_op jit(solution)/shard_map/ppermute | solution.py:346
  23.0 0.0 copy-done.2
  23.0 0.0 copy-done.3
  23.0 0.0 copy-done.4
  23.0 0.0 copy-start.5
  23.0 0.7 copy-done.5
  23.7 7.3 %score_centroids.1 = (f32[64,128]{1,0:T(8,128)}, f32[64,128]{1,0:T(8,128)}, f32[64,128]{1,0:T(8,128)}, f32[64,128]{1,0:T(8,128)}) custom-call(bf16[32,1024]{1,0:T(8,128)(2,1)} %refs_0_, bf16[32,1024]{1,0:T(8,128)(2,1)} %copy-done.2, bf16[32,1024]{1,0:T(8,128)(2,1)} %copy-done.3, bf16[32,1024]{1,0:T(8,128)(2,1)} %copy-done.4, bf16[128,1024]{1,0:T(8,128)(2,1)} %copy-done.5, ...), custom_call_target="tpu_custom_call" | custom-call | flops 2147483648 | bytes 8388608 | tf_op jit(solution)/shard_map/score_centroids/pallas_call | solution.py:232
  31.1 2.0 %collective-permute-start.4 = (f32[64,128]{1,0:T(8,128)}, f32[64,128]{1,0:T(8,128)S(1)}, u32[]{:S(2)}, u32[]{:S(2)}) collective-permute-start(f32[64,128]{1,0:T(8,128)} %get-tuple-element.33), channel_id=1, source_target_pairs={{0,6},{1,7},{2,0},{3,1},{4,2},{5,3},{6,4},{7,5},{8,14},{9,15},{10,... | collective-permute-start | bytes 98312 | tf_op jit(solution)/shard_map/ppermute | solution.py:342
  33.0 0.6 collective-permute-start.5
  33.6 0.6 collective-permute-start.6
  34.2 5.0 %all-to-all-done = bf16[128,32,128]{2,1,0:T(8,128)(2,1)S(1)} async-done(((bf16[128,32,128]{2,1,0:T(8,128)(2,1)}), bf16[128,32,128]{2,1,0:T(8,128)(2,1)S(1)}, u32[]{:S(2)}, u32[]{:S(2)}) %all-to-all-start) | async-done | bytes 1048608 | tf_op jit(solution)/shard_map/all_to_all | solution.py:337
  39.2 9.4 %score_labels.1 = bf16[12544,128]{1,0:T(8,128)(2,1)} custom-call(bf16[4096,128]{1,0:T(8,128)(2,1)S(1)} %bitcast.11, bf16[2,3072,1024]{2,1,0:T(8,128)(2,1)} %weights_ref.1), custom_call_target="tpu_custom_call" | custom-call | flops 3221225472 | bytes 12582912 | tf_op jit(solution)/shard_map/score_labels/pallas_call | solution.py:165
  48.6 0.0 collective-permute-done.4
  48.6 0.0 collective-permute-done.5
  48.6 0.0 collective-permute-done.6
  48.6 0.0 copy-start.7
  48.7 0.0 copy-start.6
  48.7 0.0 copy-start
  48.7 0.0 copy-start.1
  48.7 4.8 %all-to-all-start.1 = ((bf16[128,49,2,128]{3,2,1,0:T(2,128)(2,1)}), bf16[128,49,2,128]{3,2,1,0:T(2,128)(2,1)S(1)}, u32[]{:S(2)}, u32[]{:S(2)}) async-start(bf16[128,49,2,128]{3,2,1,0:T(2,128)(2,1)} %bitcast.12), calls=%async_computation.1 | async-start | bytes 6422528 | tf_op jit(solution)/shard_map/all_to_all | solution.py:337
  53.5 0.0 copy-done.7
  53.5 0.1 copy.5.ids_ref
  53.6 0.0 copy-done.6
  53.7 1.1 %collective-permute-start.7 = (f32[128,128]{1,0:T(8,128)S(1)}, f32[128,128]{1,0:T(8,128)S(1)}, u32[]{:S(2)}, u32[]{:S(2)}) collective-permute-start(f32[128,128]{1,0:T(8,128)S(1)} %pad_maximum_fusion.1), channel_id=1, source_target_pairs={{0,1},{1,0},{2,3},{3,2},{4,5},{5,4},{6,7},{7,6},{8,9},{9,8},{10,11... | collective-permute-start | bytes 196616 | tf_op jit(solution)/shard_map/ppermute | solution.py:346
  54.8 0.1 pad_add_fusion.owner_ref
  54.9 0.8 collective-permute-done.7.refs_4_
  55.7 1.6 %priors.1.prior_ref = f32[8,32,128]{2,1,0:T(8,128)S(1)} custom-call(s32[8]{0:T(128)S(1)} %pad_add_fusion.owner_ref, s32[32,8]{1,0:T(8,128)S(1)} %copy.5.ids_ref, f32[32,128]{1,0:T(8,128)S(1)} %get-tuple-element.42.refs_0_, f32[32,128]{1,0:T(8,128)S(1)} %get-tuple-element.49.refs_1_, f32[32,128]{1,0:T(8,128)S(1)} %get-tuple-element.46.refs_2_, ...), custom_call_target="tpu_custom_call" | custom-call | tf_op jit(solution)/shard_map/priors/pallas_call | solution.py:273
  57.4 38.4 %all-to-all-done.1 = bf16[128,49,2,128]{3,2,1,0:T(2,128)(2,1)S(1)} async-done(((bf16[128,49,2,128]{3,2,1,0:T(2,128)(2,1)}), bf16[128,49,2,128]{3,2,1,0:T(2,128)(2,1)S(1)}, u32[]{:S(2)}, u32[]{:S(2)}) %all-to-all-start.1) | async-done | bytes 3211296 | tf_op jit(solution)/shard_map/all_to_all | solution.py:337
  95.8 0.0 copy-done
  95.8 0.0 copy-done.1
  95.8 3.1 %join.1 = f32[6144,128]{1,0:T(8,128)} custom-call(s32[8,32]{1,0:T(8,128)S(1)} %copy-done, s32[8,32]{1,0:T(8,128)S(1)} %copy-done.1, f32[8,32,128]{2,1,0:T(8,128)S(1)} %priors.1.prior_ref, bf16[12544,128]{1,0:T(8,128)(2,1)S(1)} %bitcast.10), custom_call_target="tpu_custom_call" | custom-call | tf_op jit(solution)/shard_map/join/pallas_call | solution.py:319
  (4 shorter events, 0.0 us)
Async XLA Ops:
  0.0 8.5 %collective-permute-start = (bf16[32,1024]{1,0:T(8,128)(2,1)}, bf16[32,1024]{1,0:T(8,128)(2,1)S(1)}, u32[]{:S(2)}, u32[]{:S(2)}) collective-permute-start(bf16[32,1024]{1,0:T(8,128)(2,1)} %refs_0_), channel_id=1, source_target_pairs={{0,2},{1,3},{2,4},{3,5},{4,6},{5,7},{6,0},{7,1},{8,10},{9,11},{10,... | collective-permute-start | bytes 196616 | tf_op jit(solution)/shard_map/ppermute | solution.py:342
  2.0 6.5 %collective-permute-start.1 = (bf16[32,1024]{1,0:T(8,128)(2,1)}, bf16[32,1024]{1,0:T(8,128)(2,1)S(1)}, u32[]{:S(2)}, u32[]{:S(2)}) collective-permute-start(bf16[32,1024]{1,0:T(8,128)(2,1)} %refs_0_), channel_id=1, source_target_pairs={{0,4},{1,5},{2,6},{3,7},{4,0},{5,1},{6,2},{7,3},{8,12},{9,13},{10,... | collective-permute-start | bytes 196616 | tf_op jit(solution)/shard_map/ppermute | solution.py:342
  4.5 4.0 %collective-permute-start.2 = (bf16[32,1024]{1,0:T(8,128)(2,1)}, bf16[32,1024]{1,0:T(8,128)(2,1)S(1)}, u32[]{:S(2)}, u32[]{:S(2)}) collective-permute-start(bf16[32,1024]{1,0:T(8,128)(2,1)} %refs_0_), channel_id=1, source_target_pairs={{0,6},{1,7},{2,0},{3,1},{4,2},{5,3},{6,4},{7,5},{8,14},{9,15},{10,... | collective-permute-start | bytes 196616 | tf_op jit(solution)/shard_map/ppermute | solution.py:342
  8.5 14.5 %copy-start.2 = (bf16[32,1024]{1,0:T(8,128)(2,1)}, bf16[32,1024]{1,0:T(8,128)(2,1)S(1)}, u32[]{:S(2)}) copy-start(bf16[32,1024]{1,0:T(8,128)(2,1)S(1)} %collective-permute-done.refs_1_) | copy-start | bytes 196612
  8.5 14.5 %copy-start.3 = (bf16[32,1024]{1,0:T(8,128)(2,1)}, bf16[32,1024]{1,0:T(8,128)(2,1)S(1)}, u32[]{:S(2)}) copy-start(bf16[32,1024]{1,0:T(8,128)(2,1)S(1)} %collective-permute-done.1.refs_2_) | copy-start | bytes 196612
  8.5 14.5 %copy-start.4 = (bf16[32,1024]{1,0:T(8,128)(2,1)}, bf16[32,1024]{1,0:T(8,128)(2,1)S(1)}, u32[]{:S(2)}) copy-start(bf16[32,1024]{1,0:T(8,128)(2,1)S(1)} %collective-permute-done.2.refs_3_) | copy-start | bytes 196612
  8.6 30.6 %all-to-all-start = ((bf16[128,32,128]{2,1,0:T(8,128)(2,1)}), bf16[128,32,128]{2,1,0:T(8,128)(2,1)S(1)}, u32[]{:S(2)}, u32[]{:S(2)}) async-start(bf16[128,32,128]{2,1,0:T(8,128)(2,1)} %bitcast.13), calls=%async_computation | async-start | bytes 2097152 | tf_op jit(solution)/shard_map/all_to_all | solution.py:337
  20.7 2.3 %collective-permute-start.3 = (bf16[128,1024]{1,0:T(8,128)(2,1)S(1)}, bf16[128,1024]{1,0:T(8,128)(2,1)S(1)}, u32[]{:S(2)}, u32[]{:S(2)}) collective-permute-start(bf16[128,1024]{1,0:T(8,128)(2,1)S(1)} %pad_maximum_fusion), channel_id=1, source_target_pairs={{0,1},{1,0},{2,3},{3,2},{4,5},{5,4},{6,7},{7,6},{8,9},{9,8},{10,11... | collective-permute-start | bytes 786440 | tf_op jit(solution)/shard_map/ppermute | solution.py:346
  23.0 0.7 copy-start.5
  31.1 17.5 %collective-permute-start.4 = (f32[64,128]{1,0:T(8,128)}, f32[64,128]{1,0:T(8,128)S(1)}, u32[]{:S(2)}, u32[]{:S(2)}) collective-permute-start(f32[64,128]{1,0:T(8,128)} %get-tuple-element.33), channel_id=1, source_target_pairs={{0,6},{1,7},{2,0},{3,1},{4,2},{5,3},{6,4},{7,5},{8,14},{9,15},{10,... | collective-permute-start | bytes 98312 | tf_op jit(solution)/shard_map/ppermute | solution.py:342
  33.0 15.6 %collective-permute-start.5 = (f32[64,128]{1,0:T(8,128)}, f32[64,128]{1,0:T(8,128)S(1)}, u32[]{:S(2)}, u32[]{:S(2)}) collective-permute-start(f32[64,128]{1,0:T(8,128)} %get-tuple-element.34), channel_id=1, source_target_pairs={{0,4},{1,5},{2,6},{3,7},{4,0},{5,1},{6,2},{7,3},{8,12},{9,13},{10,... | collective-permute-start | bytes 98312 | tf_op jit(solution)/shard_map/ppermute | solution.py:342
  33.6 15.0 %collective-permute-start.6 = (f32[64,128]{1,0:T(8,128)}, f32[64,128]{1,0:T(8,128)S(1)}, u32[]{:S(2)}, u32[]{:S(2)}) collective-permute-start(f32[64,128]{1,0:T(8,128)} %get-tuple-element.35), channel_id=1, source_target_pairs={{0,2},{1,3},{2,4},{3,5},{4,6},{5,7},{6,0},{7,1},{8,10},{9,11},{10,... | collective-permute-start | bytes 98312 | tf_op jit(solution)/shard_map/ppermute | solution.py:342
  48.6 4.9 %copy-start.7 = (s32[32,8]{0,1:T(8,128)S(1)}, s32[32,8]{0,1:T(8,128)}, u32[]{:S(2)}) copy-start(s32[32,8]{0,1:T(8,128)} %param.6) | copy-start | bytes 3076
  48.7 5.0 %copy-start.6 = (f32[64,128]{1,0:T(8,128)S(1)}, f32[64,128]{1,0:T(8,128)}, u32[]{:S(2)}) copy-start(f32[64,128]{1,0:T(8,128)} %get-tuple-element.36) | copy-start | bytes 98308
  48.7 47.1 %copy-start = (s32[8,32]{1,0:T(8,128)S(1)}, s32[8,32]{1,0:T(8,128)}, u32[]{:S(2)}) copy-start(s32[8,32]{1,0:T(8,128)} %get-tuple-element.23.row_ref) | copy-start | bytes 3076
  48.7 47.1 %copy-start.1 = (s32[8,32]{1,0:T(8,128)S(1)}, s32[8,32]{1,0:T(8,128)}, u32[]{:S(2)}) copy-start(s32[8,32]{1,0:T(8,128)} %get-tuple-element.24.place_ref) | copy-start | bytes 3076
  48.7 47.1 %all-to-all-start.1 = ((bf16[128,49,2,128]{3,2,1,0:T(2,128)(2,1)}), bf16[128,49,2,128]{3,2,1,0:T(2,128)(2,1)S(1)}, u32[]{:S(2)}, u32[]{:S(2)}) async-start(bf16[128,49,2,128]{3,2,1,0:T(2,128)(2,1)} %bitcast.12), calls=%async_computation.1 | async-start | bytes 6422528 | tf_op jit(solution)/shard_map/all_to_all | solution.py:337
  53.7 2.0 %collective-permute-start.7 = (f32[128,128]{1,0:T(8,128)S(1)}, f32[128,128]{1,0:T(8,128)S(1)}, u32[]{:S(2)}, u32[]{:S(2)}) collective-permute-start(f32[128,128]{1,0:T(8,128)S(1)} %pad_maximum_fusion.1), channel_id=1, source_target_pairs={{0,1},{1,0},{2,3},{3,2},{4,5},{5,4},{6,7},{7,6},{8,9},{9,8},{10,11... | collective-permute-start | bytes 196616 | tf_op jit(solution)/shard_map/ppermute | solution.py:346

commit v3 on v2

--- a/solution.py
+++ b/solution.py
@@ -93,7 +93,7 @@
         for i in range(sems.shape[1]):
             part = pl.ds(i * size, size)
             pieces.append((c, i * size, pltpu.make_async_copy(weights_ref.at[c, part], w.at[c, part], sems.at[c, i])))
-    ahead = 2
+    ahead = 3
     for *_, copy in pieces[:ahead]:
         copy.start()
     spread[...] = arrived_ref[...].astype(F32)
@@ -125,18 +125,11 @@
         peak[c] = largest
         mass[c] = summed
 
-    for i, (c, first, copy) in enumerate(pieces):
-        if first == 0:
-            gather(c)
-        copy.wait()
-        for *_, later in pieces[i + ahead : i + ahead + 1]:
-            later.start()
-        for n in range(size // block):
-            product(c, first + n * block)
-
+    for c in range(held):
+        gather(c)
     lane = lax.broadcasted_iota(jnp.int32, (sources, LANES), 1)
-    packed = jnp.zeros((sources, LANES), F32)
-    for c in range(held):
+
+    def pack_totals(c, packed):
         largest = jnp.max(peak[c], axis=1, keepdims=True)
         total = largest + jnp.log(jnp.sum(mass[c] * jnp.exp(peak[c] - largest), axis=1, keepdims=True))
         for m in range(capacity):
@@ -145,6 +138,18 @@
                 term = rest.astype(BF16).astype(F32)
                 packed = jnp.where(lane == t * places + c * capacity + m, term, packed)
                 rest = rest - term
+        return packed
+
+    packed = jnp.zeros((sources, LANES), F32)
+    for i, (c, first, copy) in enumerate(pieces):
+        copy.wait()
+        for *_, later in pieces[i + ahead : i + ahead + 1]:
+            later.start()
+        for n in range(size // block):
+            product(c, first + n * block)
+        if first == 0 and c > 0:
+            packed = pack_totals(c - 1, packed)
+    packed = pack_totals(held - 1, packed)
     stage[pl.ds(places * columns, sources, stride=rows), :] = packed
     stage[pl.ds(places * columns + 1, sources, stride=rows), :] = jnp.zeros_like(packed)
     outs = []
@@ -176,7 +181,7 @@
             pltpu.VMEM((sources * rows, LANES), F32),
             pltpu.VMEM((sources * rows, LANES), BF16),
             pltpu.SemaphoreType.DMA((held, 2)),
-            pltpu.SemaphoreType.DMA((4,)),
+            pltpu.SemaphoreType.DMA((8,)),
         ],
         compiler_params=pltpu.CompilerParams(vmem_limit_bytes=50 * MIB),
         cost_estimate=pl.CostEstimate(
@@ -189,37 +194,58 @@
 
 
 def centroid_kernel(spacing, *refs):
-    chips = (len(refs) - 7) // 2
-    mine_refs, theirs_ref, centroids_ref, out_refs = refs[:chips], refs[chips], refs[chips + 1], refs[chips + 2 : -5]
-    x, w, scores, heads, sems = refs[-5:]
-    blocks, block, _ = w.shape
-    here = block // spacing
-    held = heads.shape[0]
+    chips = (len(refs) - 7) // 3
+    mine_refs, theirs_refs, centroids_ref, out_refs = (
+        refs[:chips], refs[chips : 2 * chips], refs[2 * chips], refs[2 * chips + 1 : -6],
+    )
+    x, w, peak, mass, heads, sems = refs[-6:]
+    held = w.shape[0]
+    size = held // sems.shape[0]
+    block = 512
+    pieces = []
+    for i in range(sems.shape[0]):
+        part = pl.ds(i * size, size)
+        pieces.append(pltpu.make_async_copy(centroids_ref.at[part], w.at[part], sems.at[i]))
+    ahead = 4
+    for copy in pieces[:ahead]:
+        copy.start()
     rows = mine_refs[0].shape[0]
-    copies = [
-        pltpu.make_async_copy(centroids_ref.at[pl.ds(n * block, block)], w.at[n], sems.at[n]) for n in range(blocks)
-    ]
-    for copy in copies:
-        copy.start()
-    for i, ref in enumerate(mine_refs):
-        x[2 * i * rows : (2 * i + 1) * rows, :] = ref[...]
-        x[(2 * i + 1) * rows : (2 * i + 2) * rows, :] = theirs_ref[i * rows : (i + 1) * rows, :]
-    for n in range(blocks):
-        copies[n].wait()
-        scores[:, n * block : (n + 1) * block] = lax.dot_general(
-            x[...], w[n], (((1,), (1,)), ((), ())), preferred_element_type=F32
+    for i in range(chips):
+        x[2 * i * rows : (2 * i + 1) * rows, :] = mine_refs[i][...]
+        x[(2 * i + 1) * rows : (2 * i + 2) * rows, :] = theirs_refs[i][...]
+
+    def product(first):
+        scores = lax.dot_general(
+            x[...], w[first : first + block, :], (((1,), (1,)), ((), ())), preferred_element_type=F32
         )
-        for h in range(here):
-            heads[n * here + h : n * here + h + 1, :] = w[n, h * spacing : h * spacing + 16, :].astype(F32)[0:1]
+        cuts = [scores[:, j * LANES : (j + 1) * LANES] for j in range(block // LANES)]
+        largest = functools.reduce(jnp.maximum, cuts)
+        if first > 0:
+            before = peak[...]
+            largest = jnp.maximum(largest, before)
+        summed = sum(jnp.exp(cut - largest) for cut in cuts)
+        if first > 0:
+            summed = summed + mass[...] * jnp.exp(before - largest)
+        peak[...] = largest
+        mass[...] = summed
+        for h in range(first // spacing, (first + block) // spacing):
+            heads[h : h + 1, :] = w[h * spacing : h * spacing + 16, :].astype(F32)[0:1]
+
+    for i, copy in enumerate(pieces):
+        copy.wait()
+        for later in pieces[i + ahead : i + ahead + 1]:
+            later.start()
+        for first in range(i * size, (i + 1) * size, block):
+            product(first)
     picked = lax.dot_general(x[...], heads[...].astype(BF16), (((1,), (1,)), ((), ())), preferred_element_type=F32)
-    lane = lax.broadcasted_iota(jnp.int32, (2 * rows, LANES), 1)
+    largest = jnp.max(peak[...], axis=1, keepdims=True)
+    summed = jnp.sum(mass[...] * jnp.exp(peak[...] - largest), axis=1, keepdims=True)
+    count = heads.shape[0]
+    lane = lax.broadcasted_iota(jnp.int32, peak.shape, 1)
+    padded = jnp.concatenate([picked, jnp.zeros((peak.shape[0], LANES - count), F32)], axis=1)
+    shares = jnp.where(lane == count, largest, jnp.where(lane == count + 1, summed, padded))
     for i, ref in enumerate(out_refs):
-        span = slice(2 * i * rows, 2 * (i + 1) * rows)
-        part = scores[span, :]
-        largest = jnp.max(part, axis=1, keepdims=True)
-        summed = jnp.sum(jnp.exp(part - largest), axis=1, keepdims=True)
-        padded = jnp.concatenate([picked[span], jnp.zeros((2 * rows, LANES - held), F32)], axis=1)
-        ref[...] = jnp.where(lane == held, largest, jnp.where(lane == held + 1, summed, padded))
+        ref[...] = shares[2 * i * rows : 2 * (i + 1) * rows, :]
 
 
 def score_centroids(mine, theirs, centroids, spacing):
@@ -227,26 +253,26 @@
     held = centroids.shape[0]
     chips = len(mine)
     total = 2 * rows * chips
-    blocks = 2
     whole = pl.BlockSpec(memory_space=pltpu.VMEM)
     return pl.pallas_call(
         functools.partial(centroid_kernel, spacing),
-        in_specs=[whole] * (chips + 1) + [pl.BlockSpec(memory_space=pltpu.HBM)],
+        in_specs=[whole] * (2 * chips) + [pl.BlockSpec(memory_space=pltpu.HBM)],
         out_specs=[whole] * chips,
         out_shape=[jax.ShapeDtypeStruct((2 * rows, LANES), F32)] * chips,
         scratch_shapes=[
             pltpu.VMEM((total, width), BF16),
-            pltpu.VMEM((blocks, held // blocks, width), BF16),
-            pltpu.VMEM((total, held), F32),
+            pltpu.VMEM(centroids.shape, BF16),
+            pltpu.VMEM((total, LANES), F32),
+            pltpu.VMEM((total, LANES), F32),
             pltpu.VMEM((held // spacing, width), F32),
-            pltpu.SemaphoreType.DMA((blocks,)),
+            pltpu.SemaphoreType.DMA((4,)),
         ],
-        compiler_params=pltpu.CompilerParams(vmem_limit_bytes=54 * MIB),
+        compiler_params=pltpu.CompilerParams(vmem_limit_bytes=53 * MIB),
         cost_estimate=pl.CostEstimate(
             flops=2 * total * held * width, bytes_accessed=2 * held * width, transcendentals=total * held
         ),
         name="score_centroids",
-    )(*mine, theirs, centroids)
+    )(*mine, *theirs, centroids)
 
 
 def prior_kernel(heads, owner_ref, ids_ref, *refs):
@@ -364,7 +390,7 @@
     outgoing, *mine = lax.optimization_barrier((outgoing, *mine))
     arrived = exchange(outgoing, everyone)
 
-    theirs = swap(jnp.concatenate(mine, axis=0))
+    theirs = [swap(piece) for piece in mine]
     shares = score_centroids(mine, theirs, centroids, spacing)
     arrived, _ = lax.optimization_barrier((arrived, shares[0]))
     back = [shares[0]] + [shift(share, -by) for share, by in zip(shares[1:], hops)]

time: 99.4 us -> 97.9 us (0.985)
  Pallas kernels: 24.3 us -> 21.3 us
  waiting for transfers between devices: 45.3 us -> 47.5 us
    all_to_all x2, waiting for transfers between devices: 43.3 us -> 45.5 us  [exchange(): return lax.all_to_all(x, axes, split_axis=0, concat_axis=0, tiled=True)]
    pallas_call x1, Pallas kernels: 7.34 us -> 5.36 us  [score_centroids(): pl.pallas_call(functools.partial(centroid_kernel, spacing), in_specs=[who...]
    pallas_call x1, Pallas kernels: 9.43 us -> 8.41 us  [score_labels(): pl.pallas_call(functools.partial(label_kernel, sources, capacity), in_spe...]
    ppermute x2 -> x5, starting transfers between devices: 2.29 us -> 2.91 us  [swap(): lax.ppermute(x, 'own', [(i, i ^ 1) for i in range(lax.axis_size('own'))])]
    ppermute x2 -> x5, waiting for transfers between devices: 1.99 us -> 1.98 us  [swap(): lax.ppermute(x, 'own', [(i, i ^ 1) for i in range(lax.axis_size('own'))])]
  transfers between devices with their start and end apart: 10 -> 13, of which waited for: 4 -> 7; matrix products, arithmetic and copies ran while one was open for 1% -> 0% of each run, Pallas kernels for 21% -> 19%
where the time goes in v3:
time: 97.9 us; the launch traced here: 97.6 us
  waiting for transfers between devices  47.5 us (49%)
  starting transfers between devices  27.4 us (28%)
  Pallas kernels  21.3 us (22%)
    all_to_all x2, waiting for transfers between devices, exchange(): return lax.all_to_all(x, axes, split_axis=0, concat_axis=0, tiled=True)  45.5 us
    all_to_all x2, starting transfers between devices, exchange(): return lax.all_to_all(x, axes, split_axis=0, concat_axis=0, tiled=True)  15.8 us
    ppermute x6, starting transfers between devices, shift(): lax.ppermute(x, 'own', [(i, (i + by) % owners) for i in range(owners)])  8.76 us
    pallas_call x1, Pallas kernels, score_labels(): pl.pallas_call(functools.partial(label_kernel, sources, capacity), in_spe...  8.41 us
    pallas_call x1, Pallas kernels, score_centroids(): pl.pallas_call(functools.partial(centroid_kernel, spacing), in_specs=[who...  5.36 us
    pallas_call x1, Pallas kernels, join(): pl.pallas_call(functools.partial(join_kernel, places, columns), in_specs=...  3.05 us
    ppermute x5, starting transfers between devices, swap(): lax.ppermute(x, 'own', [(i, i ^ 1) for i in range(lax.axis_size('own'))])  2.91 us
    pallas_call x1, Pallas kernels, route(): pl.pallas_call(functools.partial(route_kernel, clusters, capacity, held,...  2.84 us
  transfers between devices with their start and end apart: 13, of which 7 were waited for; matrix products, arithmetic and copies ran while one was open for 0% of the time, Pallas kernels for 19%

profile of v3, /device:TPU:1, one launch (start us, length us, event | category | flops | bytes accessed | tf_op | source)
XLA Modules:
  0.0 97.6 jit_solution(3195516003203028578)
XLA Ops:
  0.0 2.0 %collective-permute-start = (bf16[32,1024]{1,0:T(8,128)(2,1)}, bf16[32,1024]{1,0:T(8,128)(2,1)S(1)}, u32[]{:S(2)}, u32[]{:S(2)}) collective-permute-start(bf16[32,1024]{1,0:T(8,128)(2,1)} %refs_0_), channel_id=1, source_target_pairs={{0,2},{1,3},{2,4},{3,5},{4,6},{5,7},{6,0},{7,1},{8,10},{9,11},{10,... | collective-permute-start | bytes 196616 | tf_op jit(solution)/shard_map/ppermute | solution.py:368
  2.0 2.5 %collective-permute-start.1 = (bf16[32,1024]{1,0:T(8,128)(2,1)}, bf16[32,1024]{1,0:T(8,128)(2,1)S(1)}, u32[]{:S(2)}, u32[]{:S(2)}) collective-permute-start(bf16[32,1024]{1,0:T(8,128)(2,1)} %refs_0_), channel_id=1, source_target_pairs={{0,4},{1,5},{2,6},{3,7},{4,0},{5,1},{6,2},{7,3},{8,12},{9,13},{10,... | collective-permute-start | bytes 196616 | tf_op jit(solution)/shard_map/ppermute | solution.py:368
  4.5 1.2 %collective-permute-start.2 = (bf16[32,1024]{1,0:T(8,128)(2,1)}, bf16[32,1024]{1,0:T(8,128)(2,1)S(1)}, u32[]{:S(2)}, u32[]{:S(2)}) collective-permute-start(bf16[32,1024]{1,0:T(8,128)(2,1)} %refs_0_), channel_id=1, source_target_pairs={{0,6},{1,7},{2,0},{3,1},{4,2},{5,3},{6,4},{7,5},{8,14},{9,15},{10,... | collective-permute-start | bytes 196616 | tf_op jit(solution)/shard_map/ppermute | solution.py:368
  5.6 2.8 %route.1 = (bf16[4096,128]{1,0:T(8,128)(2,1)}, s32[8,32]{1,0:T(8,128)}, s32[8,32]{1,0:T(8,128)}) custom-call(bf16[32,1024]{1,0:T(8,128)(2,1)} %refs_0_, s32[8,32]{1,0:T(8,128)} %bitcast.14), custom_call_target="tpu_custom_call" | custom-call | tf_op jit(solution)/shard_map/route/pallas_call | solution.py:59
  8.5 0.0 collective-permute-done.refs_1_
  8.5 0.0 collective-permute-done.1.refs_2_
  8.5 0.0 collective-permute-done.2.refs_3_
  8.5 11.3 %all-to-all-start = ((bf16[128,32,128]{2,1,0:T(8,128)(2,1)}), bf16[128,32,128]{2,1,0:T(8,128)(2,1)S(1)}, u32[]{:S(2)}, u32[]{:S(2)}) async-start(bf16[128,32,128]{2,1,0:T(8,128)(2,1)} %bitcast.13), calls=%async_computation | async-start | bytes 2097152 | tf_op jit(solution)/shard_map/all_to_all | solution.py:363
  19.8 1.1 %collective-permute-start.3 = (bf16[32,1024]{1,0:T(8,128)(2,1)}, bf16[32,1024]{1,0:T(8,128)(2,1)S(1)}, u32[]{:S(2)}, u32[]{:S(2)}) collective-permute-start(bf16[32,1024]{1,0:T(8,128)(2,1)} %refs_0_), channel_id=1, source_target_pairs={{0,1},{1,0},{2,3},{3,2},{4,5},{5,4},{6,7},{7,6},{8,9},{9,8},{10,11... | collective-permute-start | bytes 196616 | tf_op jit(solution)/shard_map/ppermute | solution.py:372
  21.0 0.1 collective-permute-start.4
  21.1 0.4 collective-permute-start.5
  21.5 0.1 collective-permute-start.6
  21.6 0.5 collective-permute-done.3.refs_4_
  22.1 0.1 collective-permute-done.4.refs_5_
  22.2 0.2 collective-permute-done.5.refs_6_
  22.4 0.4 collective-permute-done.6.refs_7_
  22.7 0.0 copy-start
  22.7 0.8 copy-done
  23.6 5.4 %score_centroids.1 = (f32[64,128]{1,0:T(8,128)S(1)}, f32[64,128]{1,0:T(8,128)S(1)}, f32[64,128]{1,0:T(8,128)S(1)}, f32[64,128]{1,0:T(8,128)S(1)}) custom-call(bf16[32,1024]{1,0:T(8,128)(2,1)S(1)} %copy-done, bf16[32,1024]{1,0:T(8,128)(2,1)S(1)} %collective-permute-done.refs_1_, bf16[32,1024]{1,0:T(8,128)(2,1)S(1)} %collective-permute-done.1.refs_2_, ...), custom_call_target="tpu_custom_call" | custom-call | flops 2147483648 | bytes 8388608 | tf_op jit(solution)/shard_map/score_centroids/pallas_call | solution.py:257
  28.9 2.0 %collective-permute-start.7 = (f32[64,128]{1,0:T(8,128)S(1)}, f32[64,128]{1,0:T(8,128)S(1)}, u32[]{:S(2)}, u32[]{:S(2)}) collective-permute-start(f32[64,128]{1,0:T(8,128)S(1)} %get-tuple-element.33), channel_id=1, source_target_pairs={{0,6},{1,7},{2,0},{3,1},{4,2},{5,3},{6,4},{7,5},{8,14},{9,15},{10,... | collective-permute-start | bytes 98312 | tf_op jit(solution)/shard_map/ppermute | solution.py:368
  30.9 0.6 collective-permute-start.8
  31.5 0.6 collective-permute-start.9
  32.1 7.1 %all-to-all-done = bf16[128,32,128]{2,1,0:T(8,128)(2,1)S(1)} async-done(((bf16[128,32,128]{2,1,0:T(8,128)(2,1)}), bf16[128,32,128]{2,1,0:T(8,128)(2,1)S(1)}, u32[]{:S(2)}, u32[]{:S(2)}) %all-to-all-start) | async-done | bytes 1048608 | tf_op jit(solution)/shard_map/all_to_all | solution.py:363
  39.2 8.4 %score_labels.1 = bf16[12544,128]{1,0:T(8,128)(2,1)} custom-call(bf16[4096,128]{1,0:T(8,128)(2,1)S(1)} %bitcast.11, bf16[2,3072,1024]{2,1,0:T(8,128)(2,1)} %weights_ref.1), custom_call_target="tpu_custom_call" | custom-call | flops 3221225472 | bytes 12582912 | tf_op jit(solution)/shard_map/score_labels/pallas_call | solution.py:170
  47.6 0.0 collective-permute-done.7
  47.6 0.0 collective-permute-done.8
  47.6 0.0 collective-permute-done.9
  47.6 0.0 copy-start.3
  47.6 0.0 copy-start.1
  47.6 0.0 copy-start.2
  47.7 4.5 %all-to-all-start.1 = ((bf16[128,49,2,128]{3,2,1,0:T(2,128)(2,1)}), bf16[128,49,2,128]{3,2,1,0:T(2,128)(2,1)S(1)}, u32[]{:S(2)}, u32[]{:S(2)}) async-start(bf16[128,49,2,128]{3,2,1,0:T(2,128)(2,1)} %bitcast.12), calls=%async_computation.1 | async-start | bytes 6422528 | tf_op jit(solution)/shard_map/all_to_all | solution.py:363
  52.1 0.0 copy-done.3
  52.1 0.1 copy.5.ids_ref
  52.3 1.2 %collective-permute-start.10 = (f32[128,128]{1,0:T(8,128)S(1)}, f32[128,128]{1,0:T(8,128)S(1)}, u32[]{:S(2)}, u32[]{:S(2)}) collective-permute-start(f32[128,128]{1,0:T(8,128)S(1)} %pad_maximum_fusion), channel_id=1, source_target_pairs={{0,1},{1,0},{2,3},{3,2},{4,5},{5,4},{6,7},{7,6},{8,9},{9,8},{10,11... | collective-permute-start | bytes 196616 | tf_op jit(solution)/shard_map/ppermute | solution.py:372
  53.4 0.1 pad_add_fusion.owner_ref
  53.5 0.8 collective-permute-done.10.refs_4_
  54.3 1.6 %priors.1.prior_ref = f32[8,32,128]{2,1,0:T(8,128)S(1)} custom-call(s32[8]{0:T(128)S(1)} %pad_add_fusion.owner_ref, s32[32,8]{1,0:T(8,128)S(1)} %copy.5.ids_ref, f32[32,128]{1,0:T(8,128)S(1)} %get-tuple-element.42.refs_0_, f32[32,128]{1,0:T(8,128)S(1)} %get-tuple-element.49.refs_1_, f32[32,128]{1,0:T(8,128)S(1)} %get-tuple-element.46.refs_2_, ...), custom_call_target="tpu_custom_call" | custom-call | tf_op jit(solution)/shard_map/priors/pallas_call | solution.py:299
  56.0 38.4 %all-to-all-done.1 = bf16[128,49,2,128]{3,2,1,0:T(2,128)(2,1)S(1)} async-done(((bf16[128,49,2,128]{3,2,1,0:T(2,128)(2,1)}), bf16[128,49,2,128]{3,2,1,0:T(2,128)(2,1)S(1)}, u32[]{:S(2)}, u32[]{:S(2)}) %all-to-all-start.1) | async-done | bytes 3211296 | tf_op jit(solution)/shard_map/all_to_all | solution.py:363
  94.4 0.0 copy-done.1
  94.4 0.0 copy-done.2
  94.4 3.1 %join.1 = f32[6144,128]{1,0:T(8,128)} custom-call(s32[8,32]{1,0:T(8,128)S(1)} %copy-done.1, s32[8,32]{1,0:T(8,128)S(1)} %copy-done.2, f32[8,32,128]{2,1,0:T(8,128)S(1)} %priors.1.prior_ref, bf16[12544,128]{1,0:T(8,128)(2,1)S(1)} %bitcast.10), custom_call_target="tpu_custom_call" | custom-call | tf_op jit(solution)/shard_map/join/pallas_call | solution.py:345
  (4 shorter events, 0.0 us)
Async XLA Ops:
  0.0 8.5 %collective-permute-start = (bf16[32,1024]{1,0:T(8,128)(2,1)}, bf16[32,1024]{1,0:T(8,128)(2,1)S(1)}, u32[]{:S(2)}, u32[]{:S(2)}) collective-permute-start(bf16[32,1024]{1,0:T(8,128)(2,1)} %refs_0_), channel_id=1, source_target_pairs={{0,2},{1,3},{2,4},{3,5},{4,6},{5,7},{6,0},{7,1},{8,10},{9,11},{10,... | collective-permute-start | bytes 196616 | tf_op jit(solution)/shard_map/ppermute | solution.py:368
  2.0 6.5 %collective-permute-start.1 = (bf16[32,1024]{1,0:T(8,128)(2,1)}, bf16[32,1024]{1,0:T(8,128)(2,1)S(1)}, u32[]{:S(2)}, u32[]{:S(2)}) collective-permute-start(bf16[32,1024]{1,0:T(8,128)(2,1)} %refs_0_), channel_id=1, source_target_pairs={{0,4},{1,5},{2,6},{3,7},{4,0},{5,1},{6,2},{7,3},{8,12},{9,13},{10,... | collective-permute-start | bytes 196616 | tf_op jit(solution)/shard_map/ppermute | solution.py:368
  4.5 4.0 %collective-permute-start.2 = (bf16[32,1024]{1,0:T(8,128)(2,1)}, bf16[32,1024]{1,0:T(8,128)(2,1)S(1)}, u32[]{:S(2)}, u32[]{:S(2)}) collective-permute-start(bf16[32,1024]{1,0:T(8,128)(2,1)} %refs_0_), channel_id=1, source_target_pairs={{0,6},{1,7},{2,0},{3,1},{4,2},{5,3},{6,4},{7,5},{8,14},{9,15},{10,... | collective-permute-start | bytes 196616 | tf_op jit(solution)/shard_map/ppermute | solution.py:368
  8.5 30.6 %all-to-all-start = ((bf16[128,32,128]{2,1,0:T(8,128)(2,1)}), bf16[128,32,128]{2,1,0:T(8,128)(2,1)S(1)}, u32[]{:S(2)}, u32[]{:S(2)}) async-start(bf16[128,32,128]{2,1,0:T(8,128)(2,1)} %bitcast.13), calls=%async_computation | async-start | bytes 2097152 | tf_op jit(solution)/shard_map/all_to_all | solution.py:363
  19.8 2.3 %collective-permute-start.3 = (bf16[32,1024]{1,0:T(8,128)(2,1)}, bf16[32,1024]{1,0:T(8,128)(2,1)S(1)}, u32[]{:S(2)}, u32[]{:S(2)}) collective-permute-start(bf16[32,1024]{1,0:T(8,128)(2,1)} %refs_0_), channel_id=1, source_target_pairs={{0,1},{1,0},{2,3},{3,2},{4,5},{5,4},{6,7},{7,6},{8,9},{9,8},{10,11... | collective-permute-start | bytes 196616 | tf_op jit(solution)/shard_map/ppermute | solution.py:372
  21.0 1.3 %collective-permute-start.4 = (bf16[32,1024]{1,0:T(8,128)(2,1)S(1)}, bf16[32,1024]{1,0:T(8,128)(2,1)S(1)}, u32[]{:S(2)}, u32[]{:S(2)}) collective-permute-start(bf16[32,1024]{1,0:T(8,128)(2,1)S(1)} %collective-permute-done.refs_1_), channel_id=1, source_target_pairs={{0,1},{1,0},{2,3},{3,2},{4,5},{5,4},{6,7},{7,6},{8,9},{9,8},{10,11... | collective-permute-start | bytes 196616 | tf_op jit(solution)/shard_map/ppermute | solution.py:372
  21.1 1.3 %collective-permute-start.5 = (bf16[32,1024]{1,0:T(8,128)(2,1)S(1)}, bf16[32,1024]{1,0:T(8,128)(2,1)S(1)}, u32[]{:S(2)}, u32[]{:S(2)}) collective-permute-start(bf16[32,1024]{1,0:T(8,128)(2,1)S(1)} %collective-permute-done.1.refs_2_), channel_id=1, source_target_pairs={{0,1},{1,0},{2,3},{3,2},{4,5},{5,4},{6,7},{7,6},{8,9},{9,8},{10,11... | collective-permute-start | bytes 196616 | tf_op jit(solution)/shard_map/ppermute | solution.py:372
  21.5 1.3 %collective-permute-start.6 = (bf16[32,1024]{1,0:T(8,128)(2,1)S(1)}, bf16[32,1024]{1,0:T(8,128)(2,1)S(1)}, u32[]{:S(2)}, u32[]{:S(2)}) collective-permute-start(bf16[32,1024]{1,0:T(8,128)(2,1)S(1)} %collective-permute-done.2.refs_3_), channel_id=1, source_target_pairs={{0,1},{1,0},{2,3},{3,2},{4,5},{5,4},{6,7},{7,6},{8,9},{9,8},{10,11... | collective-permute-start | bytes 196616 | tf_op jit(solution)/shard_map/ppermute | solution.py:372
  22.7 0.8 copy-start
  28.9 18.6 %collective-permute-start.7 = (f32[64,128]{1,0:T(8,128)S(1)}, f32[64,128]{1,0:T(8,128)S(1)}, u32[]{:S(2)}, u32[]{:S(2)}) collective-permute-start(f32[64,128]{1,0:T(8,128)S(1)} %get-tuple-element.33), channel_id=1, source_target_pairs={{0,6},{1,7},{2,0},{3,1},{4,2},{5,3},{6,4},{7,5},{8,14},{9,15},{10,... | collective-permute-start | bytes 98312 | tf_op jit(solution)/shard_map/ppermute | solution.py:368
  30.9 16.7 %collective-permute-start.8 = (f32[64,128]{1,0:T(8,128)S(1)}, f32[64,128]{1,0:T(8,128)S(1)}, u32[]{:S(2)}, u32[]{:S(2)}) collective-permute-start(f32[64,128]{1,0:T(8,128)S(1)} %get-tuple-element.34), channel_id=1, source_target_pairs={{0,4},{1,5},{2,6},{3,7},{4,0},{5,1},{6,2},{7,3},{8,12},{9,13},{10,... | collective-permute-start | bytes 98312 | tf_op jit(solution)/shard_map/ppermute | solution.py:368
  31.5 16.1 %collective-permute-start.9 = (f32[64,128]{1,0:T(8,128)S(1)}, f32[64,128]{1,0:T(8,128)S(1)}, u32[]{:S(2)}, u32[]{:S(2)}) collective-permute-start(f32[64,128]{1,0:T(8,128)S(1)} %get-tuple-element.35), channel_id=1, source_target_pairs={{0,2},{1,3},{2,4},{3,5},{4,6},{5,7},{6,0},{7,1},{8,10},{9,11},{10,... | collective-permute-start | bytes 98312 | tf_op jit(solution)/shard_map/ppermute | solution.py:368
  47.6 4.5 %copy-start.3 = (s32[32,8]{0,1:T(8,128)S(1)}, s32[32,8]{0,1:T(8,128)}, u32[]{:S(2)}) copy-start(s32[32,8]{0,1:T(8,128)} %param.6) | copy-start | bytes 3076
  47.6 46.7 %copy-start.1 = (s32[8,32]{1,0:T(8,128)S(1)}, s32[8,32]{1,0:T(8,128)}, u32[]{:S(2)}) copy-start(s32[8,32]{1,0:T(8,128)} %get-tuple-element.23.row_ref) | copy-start | bytes 3076
  47.6 46.7 %copy-start.2 = (s32[8,32]{1,0:T(8,128)S(1)}, s32[8,32]{1,0:T(8,128)}, u32[]{:S(2)}) copy-start(s32[8,32]{1,0:T(8,128)} %get-tuple-element.24.place_ref) | copy-start | bytes 3076
  47.7 46.7 %all-to-all-start.1 = ((bf16[128,49,2,128]{3,2,1,0:T(2,128)(2,1)}), bf16[128,49,2,128]{3,2,1,0:T(2,128)(2,1)S(1)}, u32[]{:S(2)}, u32[]{:S(2)}) async-start(bf16[128,49,2,128]{3,2,1,0:T(2,128)(2,1)} %bitcast.12), calls=%async_computation.1 | async-start | bytes 6422528 | tf_op jit(solution)/shard_map/all_to_all | solution.py:363
  52.3 2.1 %collective-permute-start.10 = (f32[128,128]{1,0:T(8,128)S(1)}, f32[128,128]{1,0:T(8,128)S(1)}, u32[]{:S(2)}, u32[]{:S(2)}) collective-permute-start(f32[128,128]{1,0:T(8,128)S(1)} %pad_maximum_fusion), channel_id=1, source_target_pairs={{0,1},{1,0},{2,3},{3,2},{4,5},{5,4},{6,7},{7,6},{8,9},{9,8},{10,11... | collective-permute-start | bytes 196616 | tf_op jit(solution)/shard_map/ppermute | solution.py:372

commit v4 on v3

--- a/solution.py
+++ b/solution.py
@@ -12,7 +12,7 @@
 MIB = 1 << 20
 
 
-def route_kernel(clusters, capacity, held, columns, queries_hbm, ids_hbm, out_ref, row_ref, total_ref, queries_ref, ids_ref, stage, sems):
+def route_kernel(clusters, capacity, queries_hbm, ids_hbm, out_ref, queries_ref, ids_ref, stage, sems):
     copies = [
         pltpu.make_async_copy(ids_hbm, ids_ref, sems.at[0]),
         pltpu.make_async_copy(queries_hbm, queries_ref, sems.at[1]),
@@ -43,6 +43,21 @@
                 :, k * LANES : (k + 1) * LANES
             ]
     out_ref[...] = stage[...].astype(BF16)
+
+
+def place_kernel(clusters, capacity, held, columns, ids_ref, row_ref, total_ref):
+    beam, rows = ids_ref.shape
+    cluster = lax.broadcasted_iota(jnp.int32, (clusters, rows), 0)
+    named = [cluster == ids_ref[s : s + 1, :] for s in range(beam)]
+    hits = functools.reduce(jnp.logical_or, named)
+    earlier = lax.broadcasted_iota(jnp.int32, (rows, rows), 0) < lax.broadcasted_iota(
+        jnp.int32, (rows, rows), 1
+    )
+    before = jnp.dot(
+        jnp.where(hits, 1.0, 0.0).astype(BF16),
+        jnp.where(earlier, 1.0, 0.0).astype(BF16),
+        preferred_element_type=F32,
+    )
     rank = jnp.concatenate(
         [jnp.sum(jnp.where(n, before, 0.0), axis=0, keepdims=True) for n in named], axis=0
     )
@@ -53,16 +68,21 @@
     total_ref[...] = place * (clusters // held) + source
 
 
-def route(queries, ids, clusters, capacity, held, columns):
+def find_places(ids, clusters, capacity, held, columns):
+    return pl.pallas_call(
+        functools.partial(place_kernel, clusters, capacity, held, columns),
+        out_shape=(jax.ShapeDtypeStruct(ids.shape, jnp.int32),) * 2,
+        compiler_params=pltpu.CompilerParams(vmem_limit_bytes=4 * MIB),
+        name="places",
+    )(ids)
+
+
+def route(queries, ids, clusters, capacity):
     rows, width = queries.shape
     total = clusters * capacity * width // LANES
     return pl.pallas_call(
-        functools.partial(route_kernel, clusters, capacity, held, columns),
-        out_shape=(
-            jax.ShapeDtypeStruct((total, LANES), BF16),
-            jax.ShapeDtypeStruct(ids.shape, jnp.int32),
-            jax.ShapeDtypeStruct(ids.shape, jnp.int32),
-        ),
+        functools.partial(route_kernel, clusters, capacity),
+        out_shape=jax.ShapeDtypeStruct((total, LANES), BF16),
         in_specs=[pl.BlockSpec(memory_space=pltpu.HBM)] * 2,
         scratch_shapes=[
             pltpu.VMEM(queries.shape, BF16),
@@ -386,7 +406,7 @@
     hops = range(2, owners, 2)
 
     mine = [queries] + [shift(queries, by) for by in hops]
-    outgoing, row_of, place_of = route(queries, cluster_ids.T, clusters, capacity, held, labels // LANES)
+    outgoing = route(queries, cluster_ids.T, clusters, capacity)
     outgoing, *mine = lax.optimization_barrier((outgoing, *mine))
     arrived = exchange(outgoing, everyone)
 
@@ -396,7 +416,8 @@
     back = [shares[0]] + [shift(share, -by) for share, by in zip(shares[1:], hops)]
 
     scores = score_labels(arrived, label_weights, devices, capacity)
-    scores, *back = lax.optimization_barrier((scores, *back))
+    scores, named, *back = lax.optimization_barrier((scores, cluster_ids.T, *back))
+    row_of, place_of = find_places(named, clusters, capacity, held, labels // LANES)
     pairs = labels * held * capacity // LANES // 2 + 1
     scores_home = exchange(scores.reshape(devices, pairs, 2, LANES), everyone).reshape(scores.shape)
 

time: 97.9 us -> 98 us (level)
    pallas_call x1 -> x2, Pallas kernels: 2.84 us -> 3.09 us  [the longest x1 2.8 us: route(): pl.pallas_call(functools.partial(route_kernel, clusters, capacity), out_s...]
where the time goes in v4:
time: 98 us; the launch traced here: 97.7 us
  waiting for transfers between devices  48 us (49%)
  starting transfers between devices  27.6 us (28%)
  Pallas kernels  21.6 us (22%)
    all_to_all x2, waiting for transfers between devices, exchange(): return lax.all_to_all(x, axes, split_axis=0, concat_axis=0, tiled=True)  46.3 us
    all_to_all x2, starting transfers between devices, exchange(): return lax.all_to_all(x, axes, split_axis=0, concat_axis=0, tiled=True)  15.8 us
    ppermute x6, starting transfers between devices, shift(): lax.ppermute(x, 'own', [(i, (i + by) % owners) for i in range(owners)])  8.75 us
    pallas_call x1, Pallas kernels, score_labels(): pl.pallas_call(functools.partial(label_kernel, sources, capacity), in_spe...  8.41 us
    pallas_call x1, Pallas kernels, score_centroids(): pl.pallas_call(functools.partial(centroid_kernel, spacing), in_specs=[who...  5.37 us
    pallas_call x1, Pallas kernels, join(): pl.pallas_call(functools.partial(join_kernel, places, columns), in_specs=...  3.05 us
    ppermute x5, starting transfers between devices, swap(): lax.ppermute(x, 'own', [(i, i ^ 1) for i in range(lax.axis_size('own'))])  3.04 us
    pallas_call x1, Pallas kernels, route(): pl.pallas_call(functools.partial(route_kernel, clusters, capacity), out_s...  2.8 us
  transfers between devices with their start and end apart: 13, of which 7 were waited for; matrix products, arithmetic and copies ran while one was open for 0% of the time, Pallas kernels for 19%

profile of v4, /device:TPU:1, one launch (start us, length us, event | category | flops | bytes accessed | tf_op | source)
XLA Modules:
  0.0 97.7 jit_solution(17681820824169932225)
XLA Ops:
  0.0 0.0 copy-start
  0.0 2.0 %collective-permute-start = (bf16[32,1024]{1,0:T(8,128)(2,1)}, bf16[32,1024]{1,0:T(8,128)(2,1)S(1)}, u32[]{:S(2)}, u32[]{:S(2)}) collective-permute-start(bf16[32,1024]{1,0:T(8,128)(2,1)} %refs_0_), channel_id=1, source_target_pairs={{0,2},{1,3},{2,4},{3,5},{4,6},{5,7},{6,0},{7,1},{8,10},{9,11},{10,... | collective-permute-start | bytes 196616 | tf_op jit(solution)/shard_map/ppermute | solution.py:388
  2.0 2.5 %collective-permute-start.1 = (bf16[32,1024]{1,0:T(8,128)(2,1)}, bf16[32,1024]{1,0:T(8,128)(2,1)S(1)}, u32[]{:S(2)}, u32[]{:S(2)}) collective-permute-start(bf16[32,1024]{1,0:T(8,128)(2,1)} %refs_0_), channel_id=1, source_target_pairs={{0,4},{1,5},{2,6},{3,7},{4,0},{5,1},{6,2},{7,3},{8,12},{9,13},{10,... | collective-permute-start | bytes 196616 | tf_op jit(solution)/shard_map/ppermute | solution.py:388
  4.5 1.2 %collective-permute-start.2 = (bf16[32,1024]{1,0:T(8,128)(2,1)}, bf16[32,1024]{1,0:T(8,128)(2,1)S(1)}, u32[]{:S(2)}, u32[]{:S(2)}) collective-permute-start(bf16[32,1024]{1,0:T(8,128)(2,1)} %refs_0_), channel_id=1, source_target_pairs={{0,6},{1,7},{2,0},{3,1},{4,2},{5,3},{6,4},{7,5},{8,14},{9,15},{10,... | collective-permute-start | bytes 196616 | tf_op jit(solution)/shard_map/ppermute | solution.py:388
  5.6 2.8 %route.1 = bf16[4096,128]{1,0:T(8,128)(2,1)} custom-call(bf16[32,1024]{1,0:T(8,128)(2,1)} %refs_0_, s32[8,32]{1,0:T(8,128)} %bitcast.12), custom_call_target="tpu_custom_call" | custom-call | tf_op jit(solution)/shard_map/route/pallas_call | solution.py:83
  8.5 0.0 collective-permute-done.refs_1_
  8.5 0.0 collective-permute-done.1.refs_2_
  8.5 0.0 collective-permute-done.2.refs_3_
  8.5 11.3 %all-to-all-start = ((bf16[128,32,128]{2,1,0:T(8,128)(2,1)}), bf16[128,32,128]{2,1,0:T(8,128)(2,1)S(1)}, u32[]{:S(2)}, u32[]{:S(2)}) async-start(bf16[128,32,128]{2,1,0:T(8,128)(2,1)} %bitcast.15), calls=%async_computation | async-start | bytes 2097152 | tf_op jit(solution)/shard_map/all_to_all | solution.py:383
  19.8 0.0 copy-done
  19.8 1.1 %collective-permute-start.3 = (bf16[32,1024]{1,0:T(8,128)(2,1)S(1)}, bf16[32,1024]{1,0:T(8,128)(2,1)S(1)}, u32[]{:S(2)}, u32[]{:S(2)}) collective-permute-start(bf16[32,1024]{1,0:T(8,128)(2,1)S(1)} %copy-done), channel_id=1, source_target_pairs={{0,1},{1,0},{2,3},{3,2},{4,5},{5,4},{6,7},{7,6},{8,9},{9,8},{10,11... | collective-permute-start | bytes 196616 | tf_op jit(solution)/shard_map/ppermute | solution.py:392
  21.0 0.1 collective-permute-start.4
  21.1 0.4 collective-permute-start.5
  21.5 0.1 collective-permute-start.6
  21.6 0.3 collective-permute-done.3.refs_4_
  21.9 0.4 collective-permute-done.4.refs_5_
  22.2 0.2 collective-permute-done.5.refs_6_
  22.4 0.4 collective-permute-done.6.refs_7_
  22.8 5.4 %score_centroids.1 = (f32[64,128]{1,0:T(8,128)S(1)}, f32[64,128]{1,0:T(8,128)S(1)}, f32[64,128]{1,0:T(8,128)S(1)}, f32[64,128]{1,0:T(8,128)S(1)}) custom-call(bf16[32,1024]{1,0:T(8,128)(2,1)S(1)} %copy-done, bf16[32,1024]{1,0:T(8,128)(2,1)S(1)} %collective-permute-done.refs_1_, bf16[32,1024]{1,0:T(8,128)(2,1)S(1)} %collective-permute-done.1.refs_2_, ...), custom_call_target="tpu_custom_call" | custom-call | flops 2147483648 | bytes 8388608 | tf_op jit(solution)/shard_map/score_centroids/pallas_call | solution.py:277
  28.1 1.9 %collective-permute-start.7 = (f32[64,128]{1,0:T(8,128)S(1)}, f32[64,128]{1,0:T(8,128)S(1)}, u32[]{:S(2)}, u32[]{:S(2)}) collective-permute-start(f32[64,128]{1,0:T(8,128)S(1)} %get-tuple-element.30), channel_id=1, source_target_pairs={{0,6},{1,7},{2,0},{3,1},{4,2},{5,3},{6,4},{7,5},{8,14},{9,15},{10,... | collective-permute-start | bytes 98312 | tf_op jit(solution)/shard_map/ppermute | solution.py:388
  30.1 0.6 collective-permute-start.8
  30.7 0.6 collective-permute-start.9
  31.2 7.9 %all-to-all-done = bf16[128,32,128]{2,1,0:T(8,128)(2,1)S(1)} async-done(((bf16[128,32,128]{2,1,0:T(8,128)(2,1)}), bf16[128,32,128]{2,1,0:T(8,128)(2,1)S(1)}, u32[]{:S(2)}, u32[]{:S(2)}) %all-to-all-start) | async-done | bytes 1048608 | tf_op jit(solution)/shard_map/all_to_all | solution.py:383
  39.2 8.4 %score_labels.1 = bf16[12544,128]{1,0:T(8,128)(2,1)} custom-call(bf16[4096,128]{1,0:T(8,128)(2,1)S(1)} %bitcast.11, bf16[2,3072,1024]{2,1,0:T(8,128)(2,1)} %weights_ref.1), custom_call_target="tpu_custom_call" | custom-call | flops 3221225472 | bytes 12582912 | tf_op jit(solution)/shard_map/score_labels/pallas_call | solution.py:190
  47.6 0.0 collective-permute-done.7
  47.6 0.0 collective-permute-done.8
  47.6 0.0 collective-permute-done.9
  47.6 0.0 copy-start.1
  47.6 4.5 %all-to-all-start.1 = ((bf16[128,49,2,128]{3,2,1,0:T(2,128)(2,1)}), bf16[128,49,2,128]{3,2,1,0:T(2,128)(2,1)S(1)}, u32[]{:S(2)}, u32[]{:S(2)}) async-start(bf16[128,49,2,128]{3,2,1,0:T(2,128)(2,1)} %bitcast.14), calls=%async_computation.1 | async-start | bytes 6422528 | tf_op jit(solution)/shard_map/all_to_all | solution.py:383
  52.1 0.0 copy-done.1
  52.2 0.1 copy.5.ids_ref
  52.3 1.3 %collective-permute-start.10 = (f32[128,128]{1,0:T(8,128)S(1)}, f32[128,128]{1,0:T(8,128)S(1)}, u32[]{:S(2)}, u32[]{:S(2)}) collective-permute-start(f32[128,128]{1,0:T(8,128)S(1)} %pad_maximum_fusion), channel_id=1, source_target_pairs={{0,1},{1,0},{2,3},{3,2},{4,5},{5,4},{6,7},{7,6},{8,9},{9,8},{10,11... | collective-permute-start | bytes 196616 | tf_op jit(solution)/shard_map/ppermute | solution.py:392
  53.6 0.1 pad_add_fusion.owner_ref
  53.6 0.3 places.1
  53.9 0.5 collective-permute-done.10.refs_4_
  54.5 1.6 %priors.1.prior_ref = f32[8,32,128]{2,1,0:T(8,128)S(1)} custom-call(s32[8]{0:T(128)S(1)} %pad_add_fusion.owner_ref, s32[32,8]{1,0:T(8,128)S(1)} %copy.5.ids_ref, f32[32,128]{1,0:T(8,128)S(1)} %get-tuple-element.42.refs_0_, f32[32,128]{1,0:T(8,128)S(1)} %get-tuple-element.49.refs_1_, f32[32,128]{1,0:T(8,128)S(1)} %get-tuple-element.46.refs_2_, ...), custom_call_target="tpu_custom_call" | custom-call | tf_op jit(solution)/shard_map/priors/pallas_call | solution.py:319
  56.1 38.4 %all-to-all-done.1 = bf16[128,49,2,128]{3,2,1,0:T(2,128)(2,1)S(1)} async-done(((bf16[128,49,2,128]{3,2,1,0:T(2,128)(2,1)}), bf16[128,49,2,128]{3,2,1,0:T(2,128)(2,1)S(1)}, u32[]{:S(2)}, u32[]{:S(2)}) %all-to-all-start.1) | async-done | bytes 3211296 | tf_op jit(solution)/shard_map/all_to_all | solution.py:383
  94.5 3.0 %join.1 = f32[6144,128]{1,0:T(8,128)} custom-call(s32[8,32]{1,0:T(8,128)S(1)} %get-tuple-element.34.row_ref, s32[8,32]{1,0:T(8,128)S(1)} %get-tuple-element.35.place_ref, f32[8,32,128]{2,1,0:T(8,128)S(1)} %priors.1.prior_ref, bf16[12544,128]{1,0:T(8,128)(2,1)S(1)} %bitcast.10), custom_call_target="tpu_custom_call" | custom-call | tf_op jit(solution)/shard_map/join/pallas_call | solution.py:365
  (4 shorter events, 0.0 us)
Async XLA Ops:
  0.0 19.8 %copy-start = (bf16[32,1024]{1,0:T(8,128)(2,1)S(1)}, bf16[32,1024]{1,0:T(8,128)(2,1)}, u32[]{:S(2)}) copy-start(bf16[32,1024]{1,0:T(8,128)(2,1)} %refs_0_) | copy-start | bytes 196612
  0.0 8.5 %collective-permute-start = (bf16[32,1024]{1,0:T(8,128)(2,1)}, bf16[32,1024]{1,0:T(8,128)(2,1)S(1)}, u32[]{:S(2)}, u32[]{:S(2)}) collective-permute-start(bf16[32,1024]{1,0:T(8,128)(2,1)} %refs_0_), channel_id=1, source_target_pairs={{0,2},{1,3},{2,4},{3,5},{4,6},{5,7},{6,0},{7,1},{8,10},{9,11},{10,... | collective-permute-start | bytes 196616 | tf_op jit(solution)/shard_map/ppermute | solution.py:388
  2.0 6.4 %collective-permute-start.1 = (bf16[32,1024]{1,0:T(8,128)(2,1)}, bf16[32,1024]{1,0:T(8,128)(2,1)S(1)}, u32[]{:S(2)}, u32[]{:S(2)}) collective-permute-start(bf16[32,1024]{1,0:T(8,128)(2,1)} %refs_0_), channel_id=1, source_target_pairs={{0,4},{1,5},{2,6},{3,7},{4,0},{5,1},{6,2},{7,3},{8,12},{9,13},{10,... | collective-permute-start | bytes 196616 | tf_op jit(solution)/shard_map/ppermute | solution.py:388
  4.5 4.0 %collective-permute-start.2 = (bf16[32,1024]{1,0:T(8,128)(2,1)}, bf16[32,1024]{1,0:T(8,128)(2,1)S(1)}, u32[]{:S(2)}, u32[]{:S(2)}) collective-permute-start(bf16[32,1024]{1,0:T(8,128)(2,1)} %refs_0_), channel_id=1, source_target_pairs={{0,6},{1,7},{2,0},{3,1},{4,2},{5,3},{6,4},{7,5},{8,14},{9,15},{10,... | collective-permute-start | bytes 196616 | tf_op jit(solution)/shard_map/ppermute | solution.py:388
  8.5 30.7 %all-to-all-start = ((bf16[128,32,128]{2,1,0:T(8,128)(2,1)}), bf16[128,32,128]{2,1,0:T(8,128)(2,1)S(1)}, u32[]{:S(2)}, u32[]{:S(2)}) async-start(bf16[128,32,128]{2,1,0:T(8,128)(2,1)} %bitcast.15), calls=%async_computation | async-start | bytes 2097152 | tf_op jit(solution)/shard_map/all_to_all | solution.py:383
  19.8 2.0 %collective-permute-start.3 = (bf16[32,1024]{1,0:T(8,128)(2,1)S(1)}, bf16[32,1024]{1,0:T(8,128)(2,1)S(1)}, u32[]{:S(2)}, u32[]{:S(2)}) collective-permute-start(bf16[32,1024]{1,0:T(8,128)(2,1)S(1)} %copy-done), channel_id=1, source_target_pairs={{0,1},{1,0},{2,3},{3,2},{4,5},{5,4},{6,7},{7,6},{8,9},{9,8},{10,11... | collective-permute-start | bytes 196616 | tf_op jit(solution)/shard_map/ppermute | solution.py:392
  21.0 1.3 %collective-permute-start.4 = (bf16[32,1024]{1,0:T(8,128)(2,1)S(1)}, bf16[32,1024]{1,0:T(8,128)(2,1)S(1)}, u32[]{:S(2)}, u32[]{:S(2)}) collective-permute-start(bf16[32,1024]{1,0:T(8,128)(2,1)S(1)} %collective-permute-done.refs_1_), channel_id=1, source_target_pairs={{0,1},{1,0},{2,3},{3,2},{4,5},{5,4},{6,7},{7,6},{8,9},{9,8},{10,11... | collective-permute-start | bytes 196616 | tf_op jit(solution)/shard_map/ppermute | solution.py:392
  21.1 1.3 %collective-permute-start.5 = (bf16[32,1024]{1,0:T(8,128)(2,1)S(1)}, bf16[32,1024]{1,0:T(8,128)(2,1)S(1)}, u32[]{:S(2)}, u32[]{:S(2)}) collective-permute-start(bf16[32,1024]{1,0:T(8,128)(2,1)S(1)} %collective-permute-done.1.refs_2_), channel_id=1, source_target_pairs={{0,1},{1,0},{2,3},{3,2},{4,5},{5,4},{6,7},{7,6},{8,9},{9,8},{10,11... | collective-permute-start | bytes 196616 | tf_op jit(solution)/shard_map/ppermute | solution.py:392
  21.5 1.3 %collective-permute-start.6 = (bf16[32,1024]{1,0:T(8,128)(2,1)S(1)}, bf16[32,1024]{1,0:T(8,128)(2,1)S(1)}, u32[]{:S(2)}, u32[]{:S(2)}) collective-permute-start(bf16[32,1024]{1,0:T(8,128)(2,1)S(1)} %collective-permute-done.2.refs_3_), channel_id=1, source_target_pairs={{0,1},{1,0},{2,3},{3,2},{4,5},{5,4},{6,7},{7,6},{8,9},{9,8},{10,11... | collective-permute-start | bytes 196616 | tf_op jit(solution)/shard_map/ppermute | solution.py:392
  28.1 19.5 %collective-permute-start.7 = (f32[64,128]{1,0:T(8,128)S(1)}, f32[64,128]{1,0:T(8,128)S(1)}, u32[]{:S(2)}, u32[]{:S(2)}) collective-permute-start(f32[64,128]{1,0:T(8,128)S(1)} %get-tuple-element.30), channel_id=1, source_target_pairs={{0,6},{1,7},{2,0},{3,1},{4,2},{5,3},{6,4},{7,5},{8,14},{9,15},{10,... | collective-permute-start | bytes 98312 | tf_op jit(solution)/shard_map/ppermute | solution.py:388
  30.1 17.5 %collective-permute-start.8 = (f32[64,128]{1,0:T(8,128)S(1)}, f32[64,128]{1,0:T(8,128)S(1)}, u32[]{:S(2)}, u32[]{:S(2)}) collective-permute-start(f32[64,128]{1,0:T(8,128)S(1)} %get-tuple-element.31), channel_id=1, source_target_pairs={{0,4},{1,5},{2,6},{3,7},{4,0},{5,1},{6,2},{7,3},{8,12},{9,13},{10,... | collective-permute-start | bytes 98312 | tf_op jit(solution)/shard_map/ppermute | solution.py:388
  30.7 17.0 %collective-permute-start.9 = (f32[64,128]{1,0:T(8,128)S(1)}, f32[64,128]{1,0:T(8,128)S(1)}, u32[]{:S(2)}, u32[]{:S(2)}) collective-permute-start(f32[64,128]{1,0:T(8,128)S(1)} %get-tuple-element.32), channel_id=1, source_target_pairs={{0,2},{1,3},{2,4},{3,5},{4,6},{5,7},{6,0},{7,1},{8,10},{9,11},{10,... | collective-permute-start | bytes 98312 | tf_op jit(solution)/shard_map/ppermute | solution.py:388
  47.6 4.5 %copy-start.1 = (s32[32,8]{0,1:T(8,128)S(1)}, s32[32,8]{0,1:T(8,128)}, u32[]{:S(2)}) copy-start(s32[32,8]{0,1:T(8,128)} %param.6) | copy-start | bytes 3076
  47.6 46.9 %all-to-all-start.1 = ((bf16[128,49,2,128]{3,2,1,0:T(2,128)(2,1)}), bf16[128,49,2,128]{3,2,1,0:T(2,128)(2,1)S(1)}, u32[]{:S(2)}, u32[]{:S(2)}) async-start(bf16[128,49,2,128]{3,2,1,0:T(2,128)(2,1)} %bitcast.14), calls=%async_computation.1 | async-start | bytes 6422528 | tf_op jit(solution)/shard_map/all_to_all | solution.py:383
  52.3 2.2 %collective-permute-start.10 = (f32[128,128]{1,0:T(8,128)S(1)}, f32[128,128]{1,0:T(8,128)S(1)}, u32[]{:S(2)}, u32[]{:S(2)}) collective-permute-start(f32[128,128]{1,0:T(8,128)S(1)} %pad_maximum_fusion), channel_id=1, source_target_pairs={{0,1},{1,0},{2,3},{3,2},{4,5},{5,4},{6,7},{7,6},{8,9},{9,8},{10,11... | collective-permute-start | bytes 196616 | tf_op jit(solution)/shard_map/ppermute | solution.py:392
